TPU v7x, 256 devices: a whole 4x4x8 slice. The times are simulated.
256 devices in a mesh: strike: 16 (over x, y), depth: 16 (over z, core).
Axes of the slice: x: 4, y: 4, z: 8, core: 2. Of those that a mesh axis runs over, the one named last changes fastest.
Arguments:
- dof_values: float32 [9, 35, 32768], P(None, None, ('strike', 'depth')), may hold values from -6 to 6
- star_matrices: float32 [3, 9, 9, 32768], P(None, None, None, ('strike', 'depth')), may hold values from -2 to 2
- flux_solvers: float32 [2, 4, 9, 9, 32768], P(None, None, None, None, ('strike', 'depth')), may hold values from -1 to 1
- stiffness: float32 [3, 35, 35], replicated, may hold values from -1.5 to 1.5
- flux_local: float32 [4, 35, 35], replicated, may hold values from -1 to 1
- flux_neighbour: float32 [48, 35, 35], replicated, may hold values from -1 to 1
- flux_select: int32 [4, 32768], P(None, ('strike', 'depth')), may hold values from 0 to 47
- face_source: int32 [4, 32768], P(None, ('strike', 'depth')), may hold values from 0 to 639, as said below
- side_list: int32 [4, 32768], P(None, ('strike', 'depth')), may hold values from 0 to 127
- cluster_ids: int32 [32768], P(('strike', 'depth')), may hold values from 0 to 1, as said below
- damage: float32 [32768], P(('strike', 'depth')), may hold values from 0 to 0.5
- element_size: float32 [32768], P(('strike', 'depth')), may hold values from 1 to 9
- wave_speed: float32 [32768], P(('strike', 'depth')), may hold values from 1 to 2
- damage_rate: float32 [32768], P(('strike', 'depth')), may hold values from 0.5 to 4
Outputs:
- dof_next: float32 [9, 35, 32768], P(None, None, ('strike', 'depth'))
- damage_next: float32 [32768], P(('strike', 'depth'))
- next_step: float32 [], replicated
Inputs may be any that keep to these rules, and one draw needn't show every extreme that they name: `face_source`: within each partition's block, entries below 128 name its own elements and the others the received slots, four blocks of 128 in the order strike-1, strike+1, depth-1, depth+1; every slot is named by some face. `cluster_ids`: within each partition's block the elements of cluster 0 come first; there are from 16 to 64 of them, 64 in some partition.
All inputs are finite; a program needn't handle non-finite values.
Results may differ from a plain program's by a relative error of at most 0.0003.
Values sent between devices are 32-bit elements; how exact they have to be, the bound alone decides.
A program may use at most 128 MiB of HBM per device.

v0:
```python
import functools

import jax
import jax.numpy as jnp
from jax import lax
from jax.experimental import pallas as pl
from jax.experimental.pallas import tpu as pltpu
from jax.sharding import PartitionSpec as P

COURANT = 1.0
Q = 9
B = 35
BP = 40
E = 128
NSEL = 48
CHUNKS = 3
PER = Q // CHUNKS
MESH = pl.DeviceIdType.MESH
f32, bf16 = jnp.float32, jnp.bfloat16
ROW_OF_SLOT = (1, 0, 3, 2)


def split(x):
    high = x.astype(bf16)
    return high, (x - high.astype(f32)).astype(bf16)


def put_stack(stack, p, x, slot):
    high, low = split(x)
    columns = pl.ds(p * E, E)
    third = 2 * slot if 3 * slot <= 128 else 128
    stack[0:slot, columns] = high
    stack[slot : 2 * slot, columns] = low
    stack[third : third + slot, columns] = high


def make_stack(matrix, slot):
    high, low = split(matrix)
    high, low = high.astype(f32), low.astype(f32)
    if 3 * slot <= 128:
        return (high + pltpu.roll(high, slot, 1) + pltpu.roll(low, 2 * slot, 1)).astype(bf16)
    return jnp.concatenate([high + pltpu.roll(high, slot, 1), low], axis=1).astype(bf16)


def degree_of(index):
    return (
        (index >= 1).astype(jnp.int32)
        + (index >= 4).astype(jnp.int32)
        + (index >= 10).astype(jnp.int32)
        + (index >= 20).astype(jnp.int32)
    )


def kernel(
    n_strike,
    n_depth,
    dof_in,
    star_in,
    solver_in,
    stiff_in,
    local_in,
    flat_in,
    select_in,
    source_in,
    side_in,
    cluster_in,
    damage_in,
    size_in,
    speed_in,
    rate_in,
    dof_out,
    damage_out,
    step_out,
    dof_raw,
    dof,
    weights,
    stiff,
    flat,
    select,
    source,
    side,
    cluster,
    damage,
    size,
    speed,
    rate,
    gather_min,
    side_got,
    first,
    later,
    second,
    middle,
    got_a,
    got_b,
    series_1,
    series_2,
    series_3,
    series_4,
    wide,
    stack,
    matrix_0,
    matrix_1,
    matrix_2,
    matrix_u,
    applied,
    own_part,
    chosen,
    pick,
    remote_a,
    remote_b,
    load_sem,
    min_send,
    min_recv,
    side_send,
    side_recv,
    halo_send,
    halo_recv,
):
    s, d = lax.axis_index("strike"), lax.axis_index("depth")

    loads = [
        pltpu.make_async_copy(src, dst, load_sem.at[index])
        for index, (src, dst) in enumerate(
            [
                (damage_in, damage),
                (size_in, size),
                (speed_in, speed),
                (stiff_in, wide.at[0:3]),
                (dof_in, dof_raw),
                (star_in, weights.at[0:3]),
                (side_in, side),
                (source_in, source),
                (select_in, select),
                (local_in, wide.at[3:7]),
                (flat_in, flat),
                (solver_in, weights.at[3:11]),
                (cluster_in, cluster),
                (rate_in, rate),
            ]
        )
    ]
    for load in loads:
        load.start()

    barrier = pltpu.get_barrier_semaphore()
    for off in range(1, n_depth):
        pl.semaphore_signal(
            barrier, inc=1, device_id={"depth": lax.rem(d + off, n_depth)}, device_id_type=MESH
        )
    for off in range(1, n_strike):
        pl.semaphore_signal(
            barrier, inc=1, device_id={"strike": lax.rem(s + off, n_strike)}, device_id_type=MESH
        )

    has = (s > 0, s < n_strike - 1, d > 0, d < n_depth - 1)
    towards = (
        (s < n_strike - 1, {"strike": lax.rem(s + 1, n_strike)}),
        (s > 0, {"strike": lax.rem(s + n_strike - 1, n_strike)}),
        (d < n_depth - 1, {"depth": lax.rem(d + 1, n_depth)}),
        (d > 0, {"depth": lax.rem(d + n_depth - 1, n_depth)}),
    )

    for load in loads[0:3]:
        load.wait()
    gain = 1.0 - damage[...]

    def min_copy(stage, me, count, axis, off):
        other = lax.rem(me + off, count)
        return pltpu.make_async_remote_copy(
            src_ref=gather_min.at[stage, me],
            dst_ref=gather_min.at[stage, me],
            send_sem=min_send.at[stage, off],
            recv_sem=min_recv.at[stage, me],
            device_id={axis: other},
            device_id_type=MESH,
        )

    def min_start(stage, row):
        me, count, axis = ((d, n_depth, "depth"), (s, n_strike, "strike"))[stage % 2]
        gather_min[stage, me] = jnp.broadcast_to(row, (8, E))
        for off in range(1, count):
            min_copy(stage, me, count, axis, off).start()

    def min_finish(stage):
        me, count, axis = ((d, n_depth, "depth"), (s, n_strike, "strike"))[stage % 2]
        for off in range(1, count):
            other = lax.rem(me + off, count)
            pltpu.make_async_remote_copy(
                src_ref=gather_min.at[stage, other],
                dst_ref=gather_min.at[stage, other],
                send_sem=min_send.at[stage, off],
                recv_sem=min_recv.at[stage, other],
                device_id={axis: other},
                device_id_type=MESH,
            ).wait_recv()
        row = gather_min[stage, 0]
        for other in range(1, count):
            row = jnp.minimum(row, gather_min[stage, other])
        return row

    def min_drain(stage):
        me, count, axis = ((d, n_depth, "depth"), (s, n_strike, "strike"))[stage % 2]
        for off in range(1, count):
            min_copy(stage, me, count, axis, off).wait_send()

    def halo_copy(which, k, chunk, where):
        rows = pl.ds(chunk * PER, PER)
        return pltpu.make_async_remote_copy(
            src_ref=(first, second)[which].at[rows],
            dst_ref=(got_a, got_b)[which].at[k, rows],
            send_sem=halo_send.at[which, k, chunk],
            recv_sem=halo_recv.at[which, k, chunk],
            device_id=where,
            device_id_type=MESH,
        )

    def side_copy(k, where):
        return pltpu.make_async_remote_copy(
            src_ref=side,
            dst_ref=side_got.at[k],
            send_sem=side_send.at[k],
            recv_sem=side_recv.at[k],
            device_id=where,
            device_id_type=MESH,
        )

    for k in range(4):

        @pl.when(jnp.logical_not(has[k]))
        def _(k=k):
            got_a[k] = jnp.zeros((Q, BP, E), f32)
            got_b[k] = jnp.zeros((Q, BP, E), f32)
            side_got[k] = jnp.full((4, E), -1, jnp.int32)

    loads[6].wait()
    pl.semaphore_wait(barrier, n_depth + n_strike - 2)
    min_start(0, size[...] / (speed[...] * jnp.sqrt(gain)))
    for k in range(4):
        exists, where = towards[k]

        @pl.when(exists)
        def _(k=k, where=where):
            side_copy(k, where).start()

    sub = lax.broadcasted_iota(jnp.int32, (BP, E), 0)
    lane = lax.broadcasted_iota(jnp.int32, (BP, E), 1)
    inside = jnp.logical_and(sub < B, lane < B)
    keep = jnp.logical_and(inside, degree_of(sub) < degree_of(lane))
    loads[3].wait()
    stiff[...] = jnp.zeros((7, E, E), f32)
    for c in range(3):
        stiff[c, 0:B, 0:B] = wide[c]
        stiff[c, 0:BP, :] = jnp.where(keep, stiff[c, 0:BP, :], 0.0)
        matrix_0[c * 24 : (c + 1) * 24, :] = stiff[c, 0:24, :]
        matrix_1[c * 16 : (c + 1) * 16, :] = jnp.where(lane[0:16] < 20, stiff[c, 0:16, :], 0.0)
        matrix_2[c * 8 : (c + 1) * 8, :] = jnp.where(lane[0:8] < 10, stiff[c, 0:8, :], 0.0)
    stack[96:128, :] = jnp.zeros((32, Q * E), bf16)
    stack[176:256, :] = jnp.zeros((80, Q * E), bf16)

    def contract(rows, block):
        def body(g, sums):
            sums = list(sums)
            for p in range(Q):
                field = block(g, p)
                for q in range(Q):
                    sums[q] = sums[q] + weights[g, q, pl.ds(p, 1), :] * field
            return tuple(sums)

        return body

    factor = [gain if q < 6 else None for q in range(Q)]

    def scaled(q, x):
        return x * factor[q] if factor[q] is not None else x

    zeros = {rows: jnp.zeros((rows, E), f32) for rows in (8, 16, 24)}

    def derive(source_rows, matrix, slot, rows, target):
        for p in range(Q):
            x = source_rows(p)
            if x.shape[0] < slot:
                x = jnp.concatenate([x, jnp.zeros((slot - x.shape[0], E), f32)], axis=0)
            put_stack(stack, p, x, slot)
        depth_rows = 256 if 3 * slot > 128 else 3 * slot
        left = make_stack(matrix, slot)[:, 0 : max(depth_rows, 128)]
        if depth_rows < 128:
            left = left[:, 0:depth_rows]
        product = jnp.dot(left, stack[0:depth_rows, :], preferred_element_type=f32)
        for c in range(3):
            for p in range(Q):
                applied[c, p, 0:rows, :] = product[c * rows : (c + 1) * rows, p * E : (p + 1) * E]
        sums = lax.fori_loop(
            0,
            3,
            contract(rows, lambda g, p: applied[g, p, 0:rows, :]),
            tuple(jnp.zeros((rows, E), f32) for _ in range(Q)),
        )
        for q in range(Q):
            target[q] = -scaled(q, sums[q])

    def taylor(base, q, weight):
        whole = weight[0] * base[q]
        low = whole[0:8] + weight[1] * series_1[q, 0:8] + weight[2] * series_2[q, 0:8]
        low = low + weight[3] * series_3[q] + weight[4] * series_4[q]
        mid = whole[8:16] + weight[1] * series_1[q, 8:16] + weight[2] * series_2[q, 8:16]
        top = whole[16:24] + weight[1] * series_1[q, 16:24]
        return jnp.concatenate([low, mid, top, whole[24:BP]], axis=0)

    loads[4].wait()
    for q in range(Q):
        dof[q, 32:BP, :] = jnp.zeros((8, E), f32)
        dof[q, 0:B, :] = dof_raw[q]
    loads[5].wait()
    derive(lambda p: dof[p], matrix_0[...], 48, 24, series_1)
    row = min_finish(0)
    min_start(1, row[0:1])
    derive(lambda p: series_1[p], matrix_1[...], 32, 16, series_2)
    derive(lambda p: series_2[p], matrix_2[...], 16, 8, series_3)
    derive(lambda p: series_3[p], matrix_2[...], 16, 8, series_4)

    loads[9].wait()
    for c in range(3):
        matrix_u[c * BP : (c + 1) * BP, :] = jnp.transpose(stiff[c])[0:BP]
    for f in range(4):
        stiff[3 + f, 0:B, 0:B] = wide[3 + f]
        matrix_u[(3 + f) * BP : (4 + f) * BP, :] = -stiff[3 + f, 0:BP, :]

    step = jnp.min(min_finish(1)[0:1], axis=1, keepdims=True) * COURANT
    step = jnp.broadcast_to(step, (1, E))
    powers, value = [], 1.0
    for power in range(5):
        value = value * step / (power + 1)
        powers.append(value)
    late = [powers[k] * (2.0 ** (k + 1) - 1.0) for k in range(5)]

    for chunk in range(CHUNKS):
        for q in range(chunk * PER, (chunk + 1) * PER):
            first[q] = taylor(dof, q, powers)
        for k in range(4):
            exists, where = towards[k]

            @pl.when(exists)
            def _(k=k, where=where, chunk=chunk):
                halo_copy(0, k, chunk, where).start()

    for q in range(Q):
        later[q] = taylor(dof, q, late)

    update_matrix = make_stack(matrix_u[...], 48)

    def own_update(source_rows):
        for p in range(Q):
            x = jnp.concatenate([source_rows(p), zeros[8]], axis=0)
            put_stack(stack, p, x, 48)
        product = jnp.dot(update_matrix, stack[...], preferred_element_type=f32)
        for g in range(7):
            for p in range(Q):
                applied[g, p] = product[g * BP : (g + 1) * BP, p * E : (p + 1) * E]
        sums = lax.fori_loop(
            0,
            7,
            contract(BP, lambda g, p: applied[g, p]),
            tuple(jnp.zeros((BP, E), f32) for _ in range(Q)),
        )
        for q in range(Q):
            own_part[q] = sums[q]

    loads[11].wait()
    own_update(lambda p: first[p])

    loads[8].wait()
    loads[10].wait()
    number = lax.rem(lax.broadcasted_iota(jnp.int32, (E, E), 0), NSEL)
    usable = lax.broadcasted_iota(jnp.int32, (E, E), 0) < 2 * NSEL
    hot = jnp.concatenate(
        [
            jnp.where(jnp.logical_and(number == select[f : f + 1, :], usable), -1.0, 0.0).astype(bf16)
            for f in range(4)
        ],
        axis=1,
    )

    def choose(index, carry):
        rows = pl.ds(pl.multiple_of(index * 200, 8), 200)
        high, low = split(flat[rows, :])
        left = (high.astype(f32) + pltpu.roll(low.astype(f32), NSEL, 1)).astype(bf16)
        product = jnp.dot(left, hot, preferred_element_type=f32)
        for f in range(4):
            chosen[f, rows, :] = product[:, f * E : (f + 1) * E]
        return carry

    lax.fori_loop(0, B * BP // 200, choose, 0)

    loads[7].wait()
    place = lax.broadcasted_iota(jnp.int32, (E, E), 0)

    def one_hot(mask):
        return jnp.where(mask, 1.0, 0.0).astype(bf16)

    for f in range(4):
        columns = slice(f * E, (f + 1) * E)
        own = one_hot(place == source[f : f + 1, :])
        pick[4, 0:E, columns] = own
        pick[4, E : 2 * E, columns] = own
    for k in range(4):

        @pl.when(has[k])
        def _(k=k):
            side_copy(k, towards[k][1]).wait_recv()

        row = ROW_OF_SLOT[k]
        left = one_hot(place == side_got[k, row : row + 1, :])
        right = jnp.concatenate(
            [one_hot(place == source[f : f + 1, :] - (E + k * E)) for f in range(4)], axis=1
        )
        picked = jnp.dot(left, right, preferred_element_type=f32).astype(bf16)
        pick[k, 0:E, :] = picked
        pick[k, E : 2 * E, :] = picked

    loads[12].wait()
    coarse = jnp.where(cluster[...] != 0, 1.0, 0.0)

    def neighbour_update(which, own_field, finish):
        blocks = (got_a, got_b)[which]
        remote = (remote_a, remote_b)[which]
        for chunk in range(CHUNKS):
            rows = slice(chunk * PER, (chunk + 1) * PER)
            for k in range(4):

                @pl.when(has[k])
                def _(k=k, chunk=chunk):
                    halo_copy(which, k, chunk, towards[k][1]).wait_recv()

            total = None
            for k in range(5):
                block = blocks[k, rows] if k < 4 else own_field[rows]
                high, low = split(block.reshape(PER * BP, E))
                left = jnp.concatenate([high, low], axis=1)
                part = jnp.dot(left, pick[k], preferred_element_type=f32)
                total = part if total is None else total + part
            for f in range(4):
                here = total[:, f * E : (f + 1) * E]
                flat_rows = slice(chunk * PER * BP, (chunk + 1) * PER * BP)
                if which == 1:
                    here = here + coarse * remote_a[f, flat_rows, :]
                remote[f, flat_rows, :] = here

            def face(f, carry, chunk=chunk):
                sums = [jnp.zeros((BP, E), f32) for _ in range(PER)]
                for j in range(B):
                    matrix = chosen[f, j * BP : (j + 1) * BP, :]
                    for n in range(PER):
                        at = (chunk * PER + n) * BP + j
                        sums[n] = sums[n] + matrix * remote[f, at : at + 1, :]
                for n in range(PER):
                    applied[7 + f, chunk * PER + n] = sums[n]
                return carry

            lax.fori_loop(0, 4, face, 0)
        sums = lax.fori_loop(
            7,
            11,
            contract(BP, lambda g, p: applied[g, p]),
            tuple(own_part[q] for q in range(Q)),
        )
        for q in range(Q):
            finish(q, scaled(q, sums[q]))

    fine = coarse < 0.5

    def finish_a(q, change):
        middle[q] = jnp.where(fine, dof[q] + change, dof[q])

    neighbour_update(0, first, finish_a)

    derive(lambda p: middle[p], matrix_0[...], 48, 24, series_1)
    derive(lambda p: series_1[p], matrix_1[...], 32, 16, series_2)
    derive(lambda p: series_2[p], matrix_2[...], 16, 8, series_3)
    derive(lambda p: series_3[p], matrix_2[...], 16, 8, series_4)
    for chunk in range(CHUNKS):
        for q in range(chunk * PER, (chunk + 1) * PER):
            second[q] = jnp.where(fine, taylor(middle, q, powers), later[q])
        for k in range(4):
            exists, where = towards[k]

            @pl.when(exists)
            def _(k=k, where=where, chunk=chunk):
                halo_copy(1, k, chunk, where).start()

    energy = jnp.zeros((1, E), f32)
    for q in range(6):
        mean = (first[q, 0:1, :] + second[q, 0:1, :]) / (2.0 * step)
        energy = energy + mean * mean
    loads[13].wait()
    exposure = 2.0 * step * rate[...] * energy / (1.0 + energy)
    new_gain = gain * jnp.exp(-exposure)
    damage_out[...] = 1.0 - new_gain
    min_start(2, size[...] / (speed[...] * jnp.sqrt(new_gain)))

    own_update(lambda p: second[p] + coarse * first[p])
    row = min_finish(2)
    min_start(3, row[0:1])

    def finish_b(q, change):
        dof_out[q] = (middle[q] + change)[0:B]

    neighbour_update(1, second, finish_b)
    step_out[...] = COURANT * jnp.min(min_finish(3)[0:1], axis=1, keepdims=True)

    for stage in range(4):
        min_drain(stage)
    for k in range(4):
        exists, where = towards[k]

        @pl.when(exists)
        def _(k=k, where=where):
            side_copy(k, where).wait_send()
            for which in range(2):
                for chunk in range(CHUNKS):
                    halo_copy(which, k, chunk, where).wait_send()


def shards(
    n_strike,
    n_depth,
    dof_values,
    star_matrices,
    flux_solvers,
    stiffness,
    flux_local,
    flux_neighbour,
    flux_select,
    face_source,
    side_list,
    cluster_ids,
    damage,
    element_size,
    wave_speed,
    damage_rate,
):
    flat = jnp.pad(jnp.transpose(flux_neighbour, (2, 1, 0)), ((0, 0), (0, BP - B), (0, E - NSEL)))
    most = max(n_strike, n_depth)
    vmem = pltpu.VMEM
    dma = pltpu.SemaphoreType.DMA
    call = pl.pallas_call(
        functools.partial(kernel, n_strike, n_depth),
        out_shape=(
            jax.ShapeDtypeStruct((Q, B, E), f32),
            jax.ShapeDtypeStruct((1, E), f32),
            jax.ShapeDtypeStruct((1, 1), f32),
        ),
        in_specs=[pl.BlockSpec(memory_space=pl.ANY)] * 14,
        out_specs=tuple(pl.BlockSpec(memory_space=pltpu.VMEM) for _ in range(3)),
        scratch_shapes=[
            vmem((Q, B, E), f32),
            vmem((Q, BP, E), f32),
            vmem((11, Q, Q, E), f32),
            vmem((7, E, E), f32),
            vmem((B * BP, E), f32),
            vmem((4, E), jnp.int32),
            vmem((4, E), jnp.int32),
            vmem((4, E), jnp.int32),
            vmem((1, E), jnp.int32),
            vmem((1, E), f32),
            vmem((1, E), f32),
            vmem((1, E), f32),
            vmem((1, E), f32),
            vmem((4, most, 8, E), f32),
            vmem((4, 4, E), jnp.int32),
            vmem((Q, BP, E), f32),
            vmem((Q, BP, E), f32),
            vmem((Q, BP, E), f32),
            vmem((Q, BP, E), f32),
            vmem((4, Q, BP, E), f32),
            vmem((4, Q, BP, E), f32),
            vmem((Q, 24, E), f32),
            vmem((Q, 16, E), f32),
            vmem((Q, 8, E), f32),
            vmem((Q, 8, E), f32),
            vmem((7, B, B), f32),
            vmem((256, Q * E), bf16),
            vmem((72, E), f32),
            vmem((48, E), f32),
            vmem((24, E), f32),
            vmem((280, E), f32),
            vmem((11, Q, BP, E), f32),
            vmem((Q, BP, E), f32),
            vmem((4, B * BP, E), f32),
            vmem((5, 2 * E, 4 * E), bf16),
            vmem((4, Q * BP, E), f32),
            vmem((4, Q * BP, E), f32),
            dma((14,)),
            dma((4, most)),
            dma((4, most)),
            dma((4,)),
            dma((4,)),
            dma((2, 4, CHUNKS)),
            dma((2, 4, CHUNKS)),
        ],
        compiler_params=pltpu.CompilerParams(
            collective_id=0, has_side_effects=True, vmem_limit_bytes=32 * 1024 * 1024
        ),
    )
    row = (1, E)
    final, new_damage, next_step = call(
        dof_values,
        star_matrices,
        flux_solvers.reshape(8, Q, Q, E),
        stiffness,
        flux_local,
        flat.reshape(B * BP, E),
        flux_select,
        face_source,
        side_list,
        cluster_ids.reshape(row),
        damage.reshape(row),
        element_size.reshape(row),
        wave_speed.reshape(row),
        damage_rate.reshape(row),
    )
    return final, new_damage.reshape(E), next_step.reshape(())


def solution(mesh):
    both = ("strike", "depth")
    in_specs = (
        P(None, None, both),
        P(None, None, None, both),
        P(None, None, None, None, both),
        P(),
        P(),
        P(),
        P(None, both),
        P(None, both),
        P(None, both),
        P(both),
        P(both),
        P(both),
        P(both),
        P(both),
    )
    out_specs = (P(None, None, both), P(both), P())
    body = functools.partial(shards, mesh.shape["strike"], mesh.shape["depth"])
    return jax.shard_map(body, mesh=mesh, in_specs=in_specs, out_specs=out_specs, check_vma=False)
```

profile of v0, /device:TPU:1, one launch (start us, length us, event | category | flops | bytes accessed | tf_op | source)
XLA Modules:
  0.0 52.5 jit_solution(8080535867159535962)
XLA Ops:
  0.6 1.2 %copy.21 = f32[35,35,48]{2,1,0:T(8,128)S(1)} copy(f32[35,35,48]{2,0,1:T(8,128)} %bitcast.18) | data formatting | bytes 470400
  1.9 0.0 copy-start.10
  1.9 0.1 pad.4.clone
  1.9 0.9 %copy-done.10 = f32[2,4,9,9,128]{4,1,3,2,0:T(4,128)S(1)} copy-done((f32[2,4,9,9,128]{4,1,3,2,0:T(4,128)S(1)}, f32[2,4,9,9,128]{4,1,3,2,0:T(4,128)}, u32[]{:S(2)}) %copy-start.10) | copy-done | bytes 331800
  2.9 0.1 copy.17
  2.9 0.8 %copy-done.11 = f32[3,9,9,128]{3,0,2,1:T(4,128)S(1)} copy-done((f32[3,9,9,128]{3,0,2,1:T(4,128)S(1)}, f32[3,9,9,128]{3,0,2,1:T(4,128)}, u32[]{:S(2)}) %copy-start.11) | copy-done | bytes 124440
  3.8 0.9 %copy-done.12 = f32[4,35,35]{2,0,1:T(4,128)S(1)} copy-done((f32[4,35,35]{2,0,1:T(4,128)S(1)}, f32[4,35,35]{2,0,1:T(4,128)}, u32[]{:S(2)}) %copy-start.12) | copy-done | bytes 19624
  4.7 0.0 copy-start.3
  4.7 0.0 copy-start.2
  4.7 0.0 copy-start.5
  4.7 0.0 copy-start.6
  4.7 0.0 copy-start.7
  4.7 0.0 copy-done
  4.7 0.7 %copy-done.1 = f32[3,35,35]{2,1,0:T(8,128)S(1)} copy-done((f32[3,35,35]{2,1,0:T(8,128)S(1)}, f32[3,35,35]{2,1,0:T(8,128)}, u32[]{:S(2)}) %copy-start.1) | copy-done | bytes 14724
  5.5 0.0 copy-done.4
  5.5 0.0 copy-done.8
  5.5 0.0 copy-done.9
  5.5 0.0 copy-done.3
  5.5 0.0 copy-done.2
  5.5 0.0 copy-done.5
  5.5 0.0 copy-done.6
  5.5 44.0 %shard_map.157 = (f32[9,35,128]{2,1,0:T(8,128)S(1)}, f32[1,128]{1,0:T(1,128)S(1)}, f32[1,1]{1,0:T(1,128)}) custom-call(f32[9,35,128]{2,1,0:T(8,128)S(1)} %copy-done, f32[3,9,9,128]{3,2,1,0:T(8,128)S(1)} %copy.19.star_in, f32[8,9,9,128]{3,2,1,0:T(8,128)S(1)} %bitcast.11, f32[3,35,35]{2,1,0:T(8,128)S(1)} %copy-done.1, f32[4,35,35]{2,1,0:T(8,128)S(1)} %copy.20.local_in, ...), custom_call_target="tpu_custom_call" | custom-call | tf_op jit(solution)/shard_map/pallas_call | solution.py:605
  49.6 0.7 %copy.25 = f32[9,35,128]{2,1,0:T(8,128)} copy(f32[9,35,128]{2,1,0:T(8,128)S(1)} %get-tuple-element.12) | data formatting | bytes 322560
  50.2 0.5 copy.26
  (10 shorter events, 0.0 us)
Async XLA Ops:
  1.9 1.0 %copy-start.10 = (f32[2,4,9,9,128]{4,1,3,2,0:T(4,128)S(1)}, f32[2,4,9,9,128]{4,1,3,2,0:T(4,128)}, u32[]{:S(2)}) copy-start(f32[2,4,9,9,128]{4,1,3,2,0:T(4,128)} %param.16) | copy-start | bytes 995332
  2.8 0.9 %copy-start.11 = (f32[3,9,9,128]{3,0,2,1:T(4,128)S(1)}, f32[3,9,9,128]{3,0,2,1:T(4,128)}, u32[]{:S(2)}) copy-start(f32[3,9,9,128]{3,0,2,1:T(4,128)} %param.15) | copy-start | bytes 373252
  3.8 0.9 %copy-start.12 = (f32[4,35,35]{2,0,1:T(4,128)S(1)}, f32[4,35,35]{2,0,1:T(4,128)}, u32[]{:S(2)}) copy-start(f32[4,35,35]{2,0,1:T(4,128)} %param.18) | copy-start | bytes 58804
  3.8 1.0 %copy-start = (f32[9,35,128]{2,1,0:T(8,128)S(1)}, f32[9,35,128]{2,1,0:T(8,128)}, u32[]{:S(2)}) copy-start(f32[9,35,128]{2,1,0:T(8,128)} %dof_in.1) | copy-start | bytes 483844
  4.6 0.8 %copy-start.1 = (f32[3,35,35]{2,1,0:T(8,128)S(1)}, f32[3,35,35]{2,1,0:T(8,128)}, u32[]{:S(2)}) copy-start(f32[3,35,35]{2,1,0:T(8,128)} %stiff_in.1) | copy-start | bytes 44104
  4.7 0.8 %copy-start.4 = (s32[4,128]{1,0:T(4,128)S(1)}, s32[4,128]{1,0:T(4,128)}, u32[]{:S(2)}) copy-start(s32[4,128]{1,0:T(4,128)} %side_in.1) | copy-start | bytes 6148
  4.7 0.8 %copy-start.8 = (f32[128]{0:T(128)S(1)}, f32[128]{0:T(128)}, u32[]{:S(2)}) copy-start(f32[128]{0:T(128)} %param.26) | copy-start | bytes 1540
  4.7 0.8 %copy-start.9 = (f32[128]{0:T(128)S(1)}, f32[128]{0:T(128)}, u32[]{:S(2)}) copy-start(f32[128]{0:T(128)} %param.27) | copy-start | bytes 1540
  4.7 0.8 %copy-start.3 = (s32[4,128]{1,0:T(4,128)S(1)}, s32[4,128]{1,0:T(4,128)}, u32[]{:S(2)}) copy-start(s32[4,128]{1,0:T(4,128)} %source_in.1) | copy-start | bytes 6148
  4.7 0.8 %copy-start.2 = (s32[4,128]{1,0:T(4,128)S(1)}, s32[4,128]{1,0:T(4,128)}, u32[]{:S(2)}) copy-start(s32[4,128]{1,0:T(4,128)} %select_in.1) | copy-start | bytes 6148
  4.7 0.8 %copy-start.5 = (s32[128]{0:T(128)S(1)}, s32[128]{0:T(128)}, u32[]{:S(2)}) copy-start(s32[128]{0:T(128)} %param.23) | copy-start | bytes 1540
  4.7 0.8 %copy-start.6 = (f32[128]{0:T(128)S(1)}, f32[128]{0:T(128)}, u32[]{:S(2)}) copy-start(f32[128]{0:T(128)} %param.24) | copy-start | bytes 1540
  4.7 0.8 %copy-start.7 = (f32[128]{0:T(128)S(1)}, f32[128]{0:T(128)}, u32[]{:S(2)}) copy-start(f32[128]{0:T(128)} %param.25) | copy-start | bytes 1540
where the time goes:
time: 52.7 us; the launch traced here: 52.5 us
  Pallas kernels  44 us (83%)
  local copies, waits for them, and re-layouts  5.98 us (11%)
  between operations  2.46 us (5%)
    pallas_call x1, Pallas kernels, shards(): call(dof_values, star_matrices, flux_solvers.reshape(8, Q, Q, E), stiffne...  44 us
    unnamed x32, local copies, waits for them, and re-layouts  5.93 us

commit v1 on v0

v1 whole, which is shorter than its diff:
```python
import functools

import jax
import jax.numpy as jnp
from jax import lax
from jax.experimental import pallas as pl
from jax.experimental.pallas import tpu as pltpu
from jax.sharding import PartitionSpec as P

COURANT = 1.0
Q = 9
B = 35
BP = 40
E = 128
HALF = 64
NSEL = 48
MESH = pl.DeviceIdType.MESH
f32, bf16 = jnp.float32, jnp.bfloat16
ROW_OF_SLOT = (1, 0, 3, 2)
TERMS = ((0, 0, 35), (1, 0, 20), (1, 24, 10), (1, 20, 4), (1, 34, 1))
MARK = 35
ROWS = (40, 24, 16, 8, 8)
SLOTS = (48, 32, 16, 16, 16)


def split(x):
    high = x.astype(bf16)
    return high, (x - high.astype(f32)).astype(bf16)


def third_of(slot):
    return 2 * slot if 3 * slot <= 128 else 128


def make_stack(matrix, slot):
    lane = lax.broadcasted_iota(jnp.int32, matrix.shape, 1)
    high, low = split(jnp.where(lane < slot, matrix, 0.0))
    high, low = high.astype(f32), low.astype(f32)
    if 3 * slot <= 128:
        return (high + pltpu.roll(high, slot, 1) + pltpu.roll(low, 2 * slot, 1)).astype(bf16)
    return jnp.concatenate([high + pltpu.roll(high, slot, 1), low], axis=1).astype(bf16)


def degree_of(index):
    degree = jnp.zeros_like(index)
    for first in (1, 4, 10, 20):
        degree = degree + jnp.where(index >= first, 1, 0)
    return degree


def kernel(
    n_strike,
    n_depth,
    dof_in,
    star_in,
    solver_in,
    stiff_in,
    local_in,
    flat_in,
    select_in,
    source_in,
    side_in,
    cluster_in,
    damage_in,
    size_in,
    speed_in,
    rate_in,
    dof_out,
    damage_out,
    step_out,
    dof_raw,
    star,
    solver,
    wide_stiff,
    wide_local,
    wide_flat,
    select,
    source,
    side,
    cluster,
    damage,
    size,
    speed,
    rate,
    minima,
    side_got,
    sent_a,
    sent_b,
    got_a,
    got_b,
    series_1,
    series_2,
    series_3,
    series_4,
    first,
    second,
    middle,
    stiff,
    flat,
    fine_weights,
    stack,
    matrix_0,
    matrix_1,
    matrix_2,
    matrix_u,
    applied,
    part,
    chosen,
    pick,
    gathered,
    remote,
    load_sem,
    min_send,
    min_recv,
    side_send,
    side_recv,
    halo_send,
    halo_recv,
):
    s, d = lax.axis_index("strike"), lax.axis_index("depth")
    series = (sent_a.at[0], series_1, series_2, series_3, series_4)

    loads = [
        pltpu.make_async_copy(src, dst, load_sem.at[index])
        for index, (src, dst) in enumerate(
            [
                (damage_in, damage),
                (size_in, size),
                (speed_in, speed),
                (dof_in, dof_raw),
                (cluster_in, cluster),
                (stiff_in, wide_stiff),
                (star_in, star),
                (side_in, side),
                (solver_in, solver),
                (local_in, wide_local),
                (flat_in, wide_flat),
                (select_in, select),
                (source_in, source),
                (rate_in, rate),
            ]
        )
    ]

    barrier = pltpu.get_barrier_semaphore()
    groups = {"depth": (d, n_depth), "strike": (s, n_strike)}
    order = sorted(range(1, max(n_depth, n_strike)), key=lambda off: abs(off - n_depth / 2))
    for off in order:
        for axis, (me, count) in groups.items():
            if off < count:
                pl.semaphore_signal(
                    barrier, inc=1, device_id={axis: lax.rem(me + off, count)}, device_id_type=MESH
                )
    for load in loads:
        load.start()

    has = (s > 0, s < n_strike - 1, d > 0, d < n_depth - 1)
    towards = (
        (s < n_strike - 1, {"strike": lax.rem(s + 1, n_strike)}),
        (s > 0, {"strike": lax.rem(s + n_strike - 1, n_strike)}),
        (d < n_depth - 1, {"depth": lax.rem(d + 1, n_depth)}),
        (d > 0, {"depth": lax.rem(d + n_depth - 1, n_depth)}),
    )

    def min_copy(stage, slot, off):
        axis = ("depth", "strike")[stage % 2]
        me, count = groups[axis]
        return pltpu.make_async_remote_copy(
            src_ref=minima.at[stage, slot],
            dst_ref=minima.at[stage, slot],
            send_sem=min_send.at[stage, off],
            recv_sem=min_recv.at[stage, slot],
            device_id={axis: lax.rem(me + off, count)},
            device_id_type=MESH,
        )

    def min_offsets(stage):
        count = groups[("depth", "strike")[stage % 2]][1]
        return [off for off in order if off < count]

    def min_start(stage, row):
        me, count = groups[("depth", "strike")[stage % 2]]
        minima[stage, me] = row
        for off in min_offsets(stage):
            min_copy(stage, me, off).start()

    def min_finish(stage):
        me, count = groups[("depth", "strike")[stage % 2]]
        for off in reversed(min_offsets(stage)):
            min_copy(stage, lax.rem(me + off, count), off).wait_recv()
        rows = [minima[stage, other] for other in range(count)]
        while len(rows) > 1:
            rows = [jnp.minimum(a, b) for a, b in zip(rows[::2], rows[1::2])] + rows[len(rows) // 2 * 2 :]
        return rows[0]

    def min_drain(stage):
        me, _ = groups[("depth", "strike")[stage % 2]]
        for off in min_offsets(stage):
            min_copy(stage, me, off).wait_send()

    def halo_copy(piece, k, where):
        return pltpu.make_async_remote_copy(
            src_ref=sent_a.at[piece] if piece < 2 else sent_b,
            dst_ref=got_a.at[k, piece] if piece < 2 else got_b.at[k],
            send_sem=halo_send.at[piece, k],
            recv_sem=halo_recv.at[piece, k],
            device_id=where,
            device_id_type=MESH,
        )

    def side_copy(k, where):
        return pltpu.make_async_remote_copy(
            src_ref=side,
            dst_ref=side_got.at[k],
            send_sem=side_send.at[k],
            recv_sem=side_recv.at[k],
            device_id=where,
            device_id_type=MESH,
        )

    def to_all(send):
        for k in range(4):
            exists, where = towards[k]

            @pl.when(exists)
            def _(k=k, where=where):
                send(k, where)

    def from_all(receive):
        for k in range(4):

            @pl.when(has[k])
            def _(k=k):
                receive(k, towards[k][1])

    for k in range(4):

        @pl.when(jnp.logical_not(has[k]))
        def _(k=k):
            got_a[k] = jnp.zeros((2, Q, BP, E), f32)
            got_b[k] = jnp.zeros((5, BP, E), f32)
            side_got[k] = jnp.full((4, E), -1, jnp.int32)

    stack[96:128, :] = jnp.zeros((32, Q * E), bf16)
    stack[176:256, :] = jnp.zeros((80, Q * E), bf16)
    stiff[...] = jnp.zeros((7, E, E), f32)

    left_half = lax.broadcasted_iota(jnp.int32, (BP, E), 1) < HALF
    left_row = left_half[0:1]
    sub = lax.broadcasted_iota(jnp.int32, (BP, E), 0)
    lane = lax.broadcasted_iota(jnp.int32, (BP, E), 1)

    def swap(x):
        return pltpu.roll(x, HALF, 1)

    def twice(x):
        return jnp.where(left_half[0 : x.shape[0]], x, swap(x))

    for load in loads[0:3]:
        load.wait()
    gain = 1.0 - damage[...]
    own_ratio = size[...] / (speed[...] * jnp.sqrt(gain))

    loads[3].wait()
    loads[4].wait()
    coarse = jnp.where(cluster[...] != 0, 1.0, 0.0)
    for q in range(Q):
        sent_a[0, q, 32:BP, :] = jnp.zeros((8, E), f32)
        sent_a[0, q, 0:B, :] = dof_raw[q]
    sent_a[0, 0, MARK : MARK + 1, :] = coarse

    loads[5].wait()
    inside = jnp.logical_and(sub < B, lane < B)
    keep = jnp.logical_and(inside, degree_of(sub) < degree_of(lane))
    for c in range(3):
        stiff[c, 0:B, 0:B] = wide_stiff[c]
        kept = jnp.where(keep, stiff[c, 0:BP, :], 0.0)
        stiff[c, 0:BP, :] = kept
        matrix_0[c * 24 : (c + 1) * 24, :] = kept[0:24]
        matrix_1[c * 16 : (c + 1) * 16, :] = jnp.where(lane[0:16] < 20, kept[0:16], 0.0)
        matrix_2[c * 8 : (c + 1) * 8, :] = jnp.where(lane[0:8] < 10, kept[0:8], 0.0)

    def put_stack(source_rows, slot):
        third = third_of(slot)
        for p in range(Q):
            x = source_rows(p)
            if x.shape[0] < slot:
                x = jnp.concatenate([x, jnp.zeros((slot - x.shape[0], E), f32)], axis=0)
            high, low = split(x)
            columns = pl.ds(p * E, E)
            stack[0:slot, columns] = high
            stack[slot : 2 * slot, columns] = low
            stack[third : third + slot, columns] = high

    def stacked_dot(left, slot):
        rows = 256 if 3 * slot > 128 else 3 * slot
        return jnp.dot(left[:, 0:rows], stack[0:rows, :], preferred_element_type=f32)

    def contract(weight, pieces, rows, sums):
        def body(p, sums):
            sums = list(sums)
            for g in pieces:
                field = applied[g, p, 0:rows, :]
                for q in range(Q):
                    sums[q] = sums[q] + weight(q, p, g) * field
            return tuple(sums)

        return lax.fori_loop(0, Q, body, tuple(sums))

    def nothing(rows):
        return [jnp.zeros((rows, E), f32) for _ in range(Q)]

    def scaled(q, x, by):
        return x * by if q < 6 else x

    def star_weight(q, p, c):
        return star[q, p, c : c + 1, :]

    def fine_weight(shift):
        return lambda q, p, g: fine_weights[q, p, g + shift : g + shift + 1, :]

    def derive(source_rows, order_in, target, fine):
        matrix = (matrix_0, matrix_1, matrix_2, matrix_2)[order_in]
        rows, slot = (24, 16, 8, 8)[order_in], SLOTS[order_in]
        put_stack(source_rows, slot)
        product = stacked_dot(make_stack(matrix[...], slot), slot)
        for p in range(Q):
            pieces = [product[c * rows : (c + 1) * rows, p * E : (p + 1) * E] for c in range(3)]
            if fine:
                pieces = [jnp.where(left_half[0:rows], pieces[0], pieces[1]), pieces[2]]
            for g, piece in enumerate(pieces):
                applied[g, p, 0:rows, :] = piece
        if fine:
            sums = contract(fine_weight(0), range(2), rows, nothing(rows))
        else:
            sums = contract(star_weight, range(3), rows, nothing(rows))
        for q in range(Q):
            total = sums[q] + swap(sums[q]) if fine else sums[q]
            target[q] = -scaled(q, total, gain_fine if fine else gain)

    loads[6].wait()
    for index in range(4):
        derive(lambda p, index=index: series[index][p], index, series[index + 1], False)
    for q in range(Q):
        sent_a[1, q, 0:16, :] = series_1[q, 0:16]
        sent_a[1, q, 16:24, :] = series_1[q, 16:24] + pltpu.roll(series_3[q], 4, 0)
        sent_a[1, q, 24:32, :] = series_2[q, 0:8]
        sent_a[1, q, 32:40, :] = series_2[q, 8:16] + pltpu.roll(series_4[q], 2, 0)

    loads[7].wait()
    pl.semaphore_wait(barrier, n_depth + n_strike - 2)
    min_start(0, own_ratio)
    to_all(lambda k, where: side_copy(k, where).start())
    for piece in range(2):
        to_all(lambda k, where: halo_copy(piece, k, where).start())

    loads[8].wait()

    def pack(q, carry):
        for p in range(Q):
            rows = [star[q, p, c : c + 1, :] for c in range(3)]
            own = [solver[0, q, p, f : f + 1, :] for f in range(4)]
            other = [solver[1, q, p, f : f + 1, :] for f in range(4)]
            tile = [
                jnp.where(left_row, rows[0], swap(rows[1])),
                jnp.where(left_row, rows[2], 0.0),
                jnp.where(left_row, own[0], swap(own[1])),
                jnp.where(left_row, own[2], swap(own[3])),
                jnp.where(left_row, other[0], swap(other[1])),
                jnp.where(left_row, other[2], swap(other[3])),
                jnp.where(left_row, swap(other[0]), other[1]),
                jnp.where(left_row, swap(other[2]), other[3]),
            ]
            for r in range(8):
                fine_weights[q, p, r : r + 1, :] = tile[r]
        return carry

    lax.fori_loop(0, Q, pack, 0)
    gain_fine = twice(gain)

    loads[9].wait()
    for c in range(3):
        matrix_u[c * BP : (c + 1) * BP, :] = jnp.transpose(stiff[c])[0:BP]
    for f in range(4):
        stiff[3 + f, 0:B, 0:B] = wide_local[:, f, :]
        matrix_u[(3 + f) * BP : (4 + f) * BP, :] = -stiff[3 + f, 0:BP, :]

    def own_fine(k):
        put_stack(lambda p: twice(series[k][p]), SLOTS[k])
        product = stacked_dot(make_stack(matrix_u[...], SLOTS[k]), SLOTS[k])
        for p in range(Q):
            pieces = [product[g * BP : (g + 1) * BP, p * E : (p + 1) * E] for g in range(7)]
            applied[0, p] = jnp.where(left_half, pieces[0], pieces[1])
            applied[1, p] = pieces[2]
            applied[2, p] = jnp.where(left_half, pieces[3], pieces[4])
            applied[3, p] = jnp.where(left_half, pieces[5], pieces[6])
        sums = contract(fine_weight(0), range(4), BP, nothing(BP))
        for q in range(Q):
            part[k, q] = sums[q]

    own_fine(0)
    own_fine(1)
    own_fine(2)
    row = min_finish(0)
    min_start(1, row)
    own_fine(3)
    own_fine(4)

    def paired(ref):
        rows = [ref[f : f + 1, :] for f in range(4)]
        return [
            jnp.where(left_row, rows[0], swap(rows[1])),
            jnp.where(left_row, rows[2], swap(rows[3])),
            jnp.where(left_row, swap(rows[0]), rows[1]),
            jnp.where(left_row, swap(rows[2]), rows[3]),
        ]

    loads[11].wait()
    number = lax.rem(lax.broadcasted_iota(jnp.int32, (E, E), 0), NSEL)
    usable = lax.broadcasted_iota(jnp.int32, (E, E), 0) < 2 * NSEL
    hot = jnp.concatenate(
        [
            jnp.where(jnp.logical_and(number == row, usable), -1.0, 0.0).astype(bf16)
            for row in paired(select)
        ],
        axis=1,
    )
    loads[10].wait()
    flat[...] = jnp.zeros((B * BP, E), f32)

    def clear(j, carry):
        for g in range(4):
            chosen[g, pl.ds(pl.multiple_of(j * BP + 32, 8), 8), :] = jnp.zeros((8, E), f32)
        return carry

    lax.fori_loop(0, B, clear, 0)

    def choose(index, carry):
        for n in range(5):
            flat[pl.ds(pl.multiple_of((index * 5 + n) * BP, 8), B), 0:NSEL] = wide_flat[index * 5 + n]
        high, low = split(flat[pl.ds(pl.multiple_of(index * 200, 8), 200), :])
        left = (high.astype(f32) + pltpu.roll(low.astype(f32), NSEL, 1)).astype(bf16)
        product = jnp.dot(left, hot, preferred_element_type=f32)
        for n in range(5):
            for g in range(4):
                chosen[g, pl.ds(index * 5 + n, B, stride=BP), :] = product[
                    n * BP : n * BP + B, g * E : (g + 1) * E
                ]
        return carry

    lax.fori_loop(0, 7, choose, 0)

    loads[12].wait()
    place = lax.broadcasted_iota(jnp.int32, (E, E), 0)

    def one_hot(mask):
        return jnp.where(mask, 1.0, 0.0).astype(bf16)

    sources = paired(source)
    from_all(lambda k, where: side_copy(k, where).wait_recv())
    for k in range(5):
        right = jnp.concatenate([one_hot(place == row - (E + k * E) % (5 * E)) for row in sources], axis=1)
        if k < 4:
            row = ROW_OF_SLOT[k]
            left = one_hot(place == side_got[k, row : row + 1, :])
            right = jnp.dot(left, right, preferred_element_type=f32).astype(bf16)
        pick[k, 0:E, :] = right
        pick[k, E : 2 * E, :] = right

    def gather(blocks):
        total = None
        for k in range(5):
            high, low = split(blocks[k])
            left = jnp.concatenate([high, low], axis=1)
            value = jnp.dot(left, pick[k], preferred_element_type=f32)
            total = value if total is None else total + value
        return total

    for piece in range(2):
        from_all(lambda k, where: halo_copy(piece, k, where).wait_recv())
        for chunk in range(3):
            rows = slice(3 * chunk, 3 * chunk + 3)
            total = gather(
                [got_a[k, piece, rows].reshape(3 * BP, E) for k in range(4)]
                + [sent_a[piece, rows].reshape(3 * BP, E)]
            )
            for g in range(4):
                gathered[piece, g, chunk * 3 * BP : (chunk + 1) * 3 * BP, :] = total[:, g * E : (g + 1) * E]

    def near(source_row, count, g, row):
        sums = nothing(BP)
        for j in range(count):
            matrix = chosen[g, j * BP : (j + 1) * BP, :]
            for p in range(Q):
                sums[p] = sums[p] + matrix * source_row(p, j)
        for p in range(Q):
            applied[row, p] = sums[p]

    for k in range(5):
        block, start, count = TERMS[k]

        def face(g, carry, block=block, start=start, count=count):
            near(lambda p, j: gathered[block, g, pl.ds(p * BP + start + j, 1), :], count, g, 4 + g)
            return carry

        lax.fori_loop(0, 2, face, 0)
        sums = contract(fine_weight(0), range(4, 6), BP, [part[k, q] for q in range(Q)])
        for q in range(Q):
            part[k, q] = sums[q]

    step = jnp.min(min_finish(1), axis=1, keepdims=True) * COURANT
    step = jnp.broadcast_to(step, (1, E))
    powers, value = [], 1.0
    for power in range(5):
        value = value * step / (power + 1)
        powers.append(value)
    late = [powers[k] * (2.0 ** (k + 1) - 1.0) for k in range(5)]

    def taylor(base, q, weight):
        whole = weight[0] * base[q]
        low = whole[0:8] + weight[1] * series_1[q, 0:8] + weight[2] * series_2[q, 0:8]
        low = low + weight[3] * series_3[q] + weight[4] * series_4[q]
        mid = whole[8:16] + weight[1] * series_1[q, 8:16] + weight[2] * series_2[q, 8:16]
        top = whole[16:24] + weight[1] * series_1[q, 16:24]
        return jnp.concatenate([low, mid, top, whole[24:BP]], axis=0)

    fine = coarse < 0.5
    for q in range(Q):
        first[q] = taylor(sent_a.at[0], q, powers)
        second[q] = taylor(sent_a.at[0], q, late)
        change = powers[0] * part[0, q]
        for k in range(1, 5):
            change = change + powers[k] * part[k, q]
        change = change + swap(change)
        middle[q] = twice(sent_a[0, q]) + scaled(q, change, gain_fine)
    for index in range(4):
        base = middle if index == 0 else series[index]
        derive(lambda p, base=base: base[p], index, series[index + 1], True)
    fine_left = jnp.logical_and(fine, left_row)
    for q in range(Q):
        applied[10, q] = taylor(middle, q, powers)
    for q in range(Q):
        second[q] = jnp.where(fine_left, applied[10, q], second[q])

    energy = jnp.zeros((1, E), f32)
    for q in range(6):
        mean = (first[q, 0:1, :] + second[q, 0:1, :]) / (2.0 * step)
        energy = energy + mean * mean
    loads[13].wait()
    exposure = 2.0 * step * rate[...] * energy / (1.0 + energy)
    new_gain = gain * jnp.exp(-exposure)
    min_start(2, size[...] / (speed[...] * jnp.sqrt(new_gain)))
    damage_out[...] = 1.0 - new_gain

    fine_both = twice(jnp.where(fine, 1.0, 0.0))
    for n in range(5):
        other = applied[10, 2 * n + 1] if n < 4 else jnp.zeros((BP, E), f32)
        sent_b[n] = jnp.where(left_half, applied[10, 2 * n], other) * fine_both
    to_all(lambda k, where: halo_copy(2, k, where).start())

    put_stack(lambda p: second[p] + coarse * first[p], 48)
    product = stacked_dot(make_stack(matrix_u[...], 48), 48)
    for g in range(7):
        for p in range(Q):
            applied[g, p] = product[g * BP : (g + 1) * BP, p * E : (p + 1) * E]

    def own_weight(q, p, g):
        return star[q, p, g : g + 1, :] if g < 3 else solver[0, q, p, g - 3 : g - 2, :]

    sums = contract(own_weight, range(7), BP, nothing(BP))
    for q in range(Q):
        part[0, q] = sums[q]
    for q in range(Q):
        base = jnp.where(fine_left, middle[q], sent_a[0, q])
        middle[q] = base

    coarse_halves = [
        jnp.where(left_row, coarse, swap(coarse)),
        jnp.where(left_row, swap(coarse), coarse),
    ]
    sub8 = lax.broadcasted_iota(jnp.int32, (8, E), 0)
    for g in range(4):
        theirs = gathered[0, g, MARK : MARK + 1, :]
        weight = [late[k] * theirs + powers[k] * coarse_halves[g // 2] for k in range(5)]
        for p in range(Q):
            low = [gathered[0, g, p * BP + 8 * t : p * BP + 8 * t + 8, :] for t in range(5)]
            high = [gathered[1, g, p * BP + 8 * t : p * BP + 8 * t + 8, :] for t in range(5)]
            value = [weight[0] * x for x in low]
            d_3 = jnp.where(sub8 < 4, pltpu.roll(high[2], 4, 0), 0.0)
            d_4 = jnp.where(sub8 < 1, pltpu.roll(high[4], 6, 0), 0.0)
            value[0] = value[0] + weight[1] * high[0] + weight[2] * high[3] + weight[3] * d_3 + weight[4] * d_4
            value[1] = value[1] + weight[1] * high[1] + weight[2] * jnp.where(sub8 < 2, high[4], 0.0)
            value[2] = value[2] + weight[1] * jnp.where(sub8 < 4, high[2], 0.0)
            for t in range(5):
                remote[g, p * BP + 8 * t : p * BP + 8 * t + 8, :] = value[t]

    for k in range(5):
        pick[k, HALF:E, :] = jnp.zeros((HALF, 4 * E), bf16)
        pick[k, E + HALF : 2 * E, :] = jnp.zeros((HALF, 4 * E), bf16)

    row = min_finish(2)
    min_start(3, row)
    from_all(lambda k, where: halo_copy(2, k, where).wait_recv())
    for n in range(5):
        blocks = [got_b[k, n] for k in range(4)] + [sent_b[n]]
        total = gather([jnp.concatenate([x, swap(x)], axis=0) for x in blocks])
        for half in range(2 if n < 4 else 1):
            rows = slice((2 * n + half) * BP, (2 * n + half + 1) * BP)
            for g in range(4):
                value = total[half * BP : (half + 1) * BP, g * E : (g + 1) * E]
                remote[g, rows, :] = remote[g, rows, :] + value

    def last_face(g, carry):
        near(lambda p, j: remote[g, p * BP + j : p * BP + j + 1, :], B, g, g)
        return carry

    lax.fori_loop(0, 4, last_face, 0)
    left_sums = contract(fine_weight(4), range(2), BP, nothing(BP))
    for q in range(Q):
        total = left_sums[q]
        part[1, q] = total + swap(total)
    right_sums = contract(fine_weight(4), range(2, 4), BP, nothing(BP))
    for q in range(Q):
        total = right_sums[q]
        value = part[0, q] + jnp.where(left_half, part[1, q], total + swap(total))
        dof_out[q] = (middle[q] + scaled(q, value, gain))[0:B]

    step_out[...] = COURANT * jnp.min(min_finish(3), axis=1, keepdims=True)

    for stage in range(4):
        min_drain(stage)

    def drain(k, where):
        side_copy(k, where).wait_send()
        for piece in range(3):
            halo_copy(piece, k, where).wait_send()

    to_all(drain)


def shards(
    n_strike,
    n_depth,
    dof_values,
    star_matrices,
    flux_solvers,
    stiffness,
    flux_local,
    flux_neighbour,
    flux_select,
    face_source,
    side_list,
    cluster_ids,
    damage,
    element_size,
    wave_speed,
    damage_rate,
):
    most = max(n_strike, n_depth)
    vmem = pltpu.VMEM
    dma = pltpu.SemaphoreType.DMA
    call = pl.pallas_call(
        functools.partial(kernel, n_strike, n_depth),
        out_shape=(
            jax.ShapeDtypeStruct((Q, B, E), f32),
            jax.ShapeDtypeStruct((1, E), f32),
            jax.ShapeDtypeStruct((1, 1), f32),
        ),
        in_specs=[pl.BlockSpec(memory_space=pltpu.HBM)] * 14,
        out_specs=tuple(pl.BlockSpec(memory_space=pltpu.VMEM) for _ in range(3)),
        scratch_shapes=[
            vmem((Q, B, E), f32),
            vmem((Q, Q, 3, E), f32),
            vmem((2, Q, Q, 4, E), f32),
            vmem((3, B, B), f32),
            vmem((B, 4, B), f32),
            vmem((B, B, NSEL), f32),
            vmem((4, E), jnp.int32),
            vmem((4, E), jnp.int32),
            vmem((4, E), jnp.int32),
            vmem((1, E), jnp.int32),
            vmem((1, E), f32),
            vmem((1, E), f32),
            vmem((1, E), f32),
            vmem((1, E), f32),
            vmem((4, most, 1, E), f32),
            vmem((4, 4, E), jnp.int32),
            vmem((2, Q, BP, E), f32),
            vmem((5, BP, E), f32),
            vmem((4, 2, Q, BP, E), f32),
            vmem((4, 5, BP, E), f32),
            vmem((Q, 24, E), f32),
            vmem((Q, 16, E), f32),
            vmem((Q, 8, E), f32),
            vmem((Q, 8, E), f32),
            vmem((Q, BP, E), f32),
            vmem((Q, BP, E), f32),
            vmem((Q, BP, E), f32),
            vmem((7, E, E), f32),
            vmem((B * BP, E), f32),
            vmem((Q, Q, 8, E), f32),
            vmem((256, Q * E), bf16),
            vmem((72, E), f32),
            vmem((48, E), f32),
            vmem((24, E), f32),
            vmem((280, E), f32),
            vmem((11, Q, BP, E), f32),
            vmem((5, Q, BP, E), f32),
            vmem((4, B * BP, E), f32),
            vmem((5, 2 * E, 4 * E), bf16),
            vmem((2, 4, Q * BP, E), f32),
            vmem((4, Q * BP, E), f32),
            dma((14,)),
            dma((4, most)),
            dma((4, most)),
            dma((4,)),
            dma((4,)),
            dma((3, 4)),
            dma((3, 4)),
        ],
        compiler_params=pltpu.CompilerParams(
            collective_id=0, has_side_effects=True, vmem_limit_bytes=32 * 1024 * 1024
        ),
    )
    row = (1, E)
    final, new_damage, next_step = call(
        dof_values,
        jnp.transpose(star_matrices, (1, 2, 0, 3)),
        jnp.transpose(flux_solvers, (0, 2, 3, 1, 4)),
        stiffness,
        jnp.transpose(flux_local, (1, 0, 2)),
        jnp.transpose(flux_neighbour, (1, 2, 0)),
        flux_select,
        face_source,
        side_list,
        cluster_ids.reshape(row),
        damage.reshape(row),
        element_size.reshape(row),
        wave_speed.reshape(row),
        damage_rate.reshape(row),
    )
    return final, new_damage.reshape(E), next_step.reshape(())


def solution(mesh):
    both = ("strike", "depth")
    in_specs = (
        P(None, None, both),
        P(None, None, None, both),
        P(None, None, None, None, both),
        P(),
        P(),
        P(),
        P(None, both),
        P(None, both),
        P(None, both),
        P(both),
        P(both),
        P(both),
        P(both),
        P(both),
    )
    out_specs = (P(None, None, both), P(both), P())
    body = functools.partial(shards, mesh.shape["strike"], mesh.shape["depth"])
    return jax.shard_map(body, mesh=mesh, in_specs=in_specs, out_specs=out_specs, check_vma=False)
```

time: 52.7 us -> 48.4 us (0.918)
  Pallas kernels: 44 us -> 38.1 us
  local copies, waits for them, and re-layouts: 5.98 us -> 7.52 us
    pallas_call x1, Pallas kernels: 44 us -> 38.1 us  [shards(): call(dof_values, jnp.transpose(star_matrices, (1, 2, 0, 3)), jnp.transpos...]
    unnamed x32 -> x30, local copies, waits for them, and re-layouts: 5.93 us -> 7.52 us
where the time goes in v1:
time: 48.4 us; the launch traced here: 48.1 us
  Pallas kernels  38.1 us (79%)
  local copies, waits for them, and re-layouts  7.52 us (16%)
  between operations  2.48 us (5%)
    pallas_call x1, Pallas kernels, shards(): call(dof_values, jnp.transpose(star_matrices, (1, 2, 0, 3)), jnp.transpos...  38.1 us
    unnamed x30, local copies, waits for them, and re-layouts  7.52 us

profile of v1, /device:TPU:1, one launch (start us, length us, event | category | flops | bytes accessed | tf_op | source)
XLA Modules:
  0.0 48.1 jit_solution(5402756767288546932)
XLA Ops:
  0.6 0.0 copy-start.12
  0.6 0.0 copy-start.13
  0.7 0.0 copy-start.8
  0.7 0.0 copy-start.7
  0.7 0.0 copy-start.6
  0.7 0.0 copy-start.9
  0.7 0.0 copy-start.10
  0.7 0.0 copy-start.11
  0.7 0.6 %copy-done.12 = f32[128]{0:T(128)S(1)} copy-done((f32[128]{0:T(128)S(1)}, f32[128]{0:T(128)}, u32[]{:S(2)}) %copy-start.12) | copy-done | bytes 536
  1.3 0.0 copy-done.13
  1.3 0.0 copy-done.8
  1.4 0.0 copy-done.7
  1.4 0.0 copy-done.6
  1.4 0.0 copy-done.9
  1.4 0.0 copy-done.11
  1.4 1.1 %copy-done = f32[48,35,35]{0,2,1:T(8,128)S(1)} copy-done((f32[48,35,35]{0,2,1:T(8,128)S(1)}, f32[48,35,35]{0,2,1:T(8,128)}, u32[]{:S(2)}) %copy-start) | copy-done | bytes 235224
  2.5 1.0 %copy-done.1 = f32[2,4,9,9,128]{4,1,3,2,0:T(4,128)S(1)} copy-done((f32[2,4,9,9,128]{4,1,3,2,0:T(4,128)S(1)}, f32[2,4,9,9,128]{4,1,3,2,0:T(4,128)}, u32[]{:S(2)}) %copy-start.1) | copy-done | bytes 331800
  3.5 0.9 %copy-done.2 = f32[9,35,128]{2,1,0:T(8,128)S(1)} copy-done((f32[9,35,128]{2,1,0:T(8,128)S(1)}, f32[9,35,128]{2,1,0:T(8,128)}, u32[]{:S(2)}) %copy-start.2) | copy-done | bytes 161304
  4.4 0.9 %copy-done.3 = f32[3,9,9,128]{3,0,2,1:T(4,128)S(1)} copy-done((f32[3,9,9,128]{3,0,2,1:T(4,128)S(1)}, f32[3,9,9,128]{3,0,2,1:T(4,128)}, u32[]{:S(2)}) %copy-start.3) | copy-done | bytes 124440
  5.3 0.9 %copy-done.4 = f32[4,35,35]{2,0,1:T(4,128)S(1)} copy-done((f32[4,35,35]{2,0,1:T(4,128)S(1)}, f32[4,35,35]{2,0,1:T(4,128)}, u32[]{:S(2)}) %copy-start.4) | copy-done | bytes 19624
  6.2 0.8 %copy-done.5 = f32[3,35,35]{2,1,0:T(8,128)S(1)} copy-done((f32[3,35,35]{2,1,0:T(8,128)S(1)}, f32[3,35,35]{2,1,0:T(8,128)}, u32[]{:S(2)}) %copy-start.5) | copy-done | bytes 14724
  7.0 38.1 %shard_map.157 = (f32[9,35,128]{2,1,0:T(8,128)S(1)}, f32[1,128]{1,0:T(1,128)S(1)}, f32[1,1]{1,0:T(1,128)}) custom-call(f32[9,35,128]{2,1,0:T(8,128)S(1)} %copy-done.2, f32[9,9,3,128]{3,2,1,0:T(4,128)S(1)} %bitcast.13, f32[2,9,9,4,128]{4,3,2,1,0:T(4,128)S(1)} %bitcast.12, f32[3,35,35]{2,1,0:T(8,128)S(1)} %copy-done.5, f32[35,4,35]{2,1,0:T(4,128)S(1)} %bitcast.14, ...), custom_call_target="tpu_custom_call" | custom-call | tf_op jit(solution)/shard_map/pallas_call | solution.py:726
  45.1 0.7 %copy.20 = f32[9,35,128]{2,1,0:T(8,128)} copy(f32[9,35,128]{2,1,0:T(8,128)S(1)} %get-tuple-element.12) | data formatting | bytes 322560
  45.8 0.5 %copy.21 = f32[128]{0:T(128)} copy(f32[128]{0:T(128)S(1)} %bitcast.20) | data formatting | bytes 1024
  (7 shorter events, 0.0 us)
Async XLA Ops:
  0.6 0.7 %copy-start.12 = (f32[128]{0:T(128)S(1)}, f32[128]{0:T(128)}, u32[]{:S(2)}) copy-start(f32[128]{0:T(128)} %param.26) | copy-start | bytes 1540
  0.6 0.7 %copy-start.13 = (f32[128]{0:T(128)S(1)}, f32[128]{0:T(128)}, u32[]{:S(2)}) copy-start(f32[128]{0:T(128)} %param.27) | copy-start | bytes 1540
  0.7 0.7 %copy-start.8 = (s32[4,128]{1,0:T(4,128)S(1)}, s32[4,128]{1,0:T(4,128)}, u32[]{:S(2)}) copy-start(s32[4,128]{1,0:T(4,128)} %side_in.1) | copy-start | bytes 6148
  0.7 0.7 %copy-start.7 = (s32[4,128]{1,0:T(4,128)S(1)}, s32[4,128]{1,0:T(4,128)}, u32[]{:S(2)}) copy-start(s32[4,128]{1,0:T(4,128)} %source_in.1) | copy-start | bytes 6148
  0.7 0.7 %copy-start.6 = (s32[4,128]{1,0:T(4,128)S(1)}, s32[4,128]{1,0:T(4,128)}, u32[]{:S(2)}) copy-start(s32[4,128]{1,0:T(4,128)} %select_in.1) | copy-start | bytes 6148
  0.7 0.7 %copy-start.9 = (s32[128]{0:T(128)S(1)}, s32[128]{0:T(128)}, u32[]{:S(2)}) copy-start(s32[128]{0:T(128)} %param.23) | copy-start | bytes 1540
  0.7 0.7 %copy-start.10 = (f32[128]{0:T(128)S(1)}, f32[128]{0:T(128)}, u32[]{:S(2)}) copy-start(f32[128]{0:T(128)} %param.24) | copy-start | bytes 1540
  0.7 0.7 %copy-start.11 = (f32[128]{0:T(128)S(1)}, f32[128]{0:T(128)}, u32[]{:S(2)}) copy-start(f32[128]{0:T(128)} %param.25) | copy-start | bytes 1540
  1.4 1.1 %copy-start = (f32[48,35,35]{0,2,1:T(8,128)S(1)}, f32[48,35,35]{0,2,1:T(8,128)}, u32[]{:S(2)}) copy-start(f32[48,35,35]{0,2,1:T(8,128)} %param.19) | copy-start | bytes 705604
  2.5 1.0 %copy-start.1 = (f32[2,4,9,9,128]{4,1,3,2,0:T(4,128)S(1)}, f32[2,4,9,9,128]{4,1,3,2,0:T(4,128)}, u32[]{:S(2)}) copy-start(f32[2,4,9,9,128]{4,1,3,2,0:T(4,128)} %param.16) | copy-start | bytes 995332
  3.5 0.9 %copy-start.2 = (f32[9,35,128]{2,1,0:T(8,128)S(1)}, f32[9,35,128]{2,1,0:T(8,128)}, u32[]{:S(2)}) copy-start(f32[9,35,128]{2,1,0:T(8,128)} %dof_in.1) | copy-start | bytes 483844
  4.4 0.9 %copy-start.3 = (f32[3,9,9,128]{3,0,2,1:T(4,128)S(1)}, f32[3,9,9,128]{3,0,2,1:T(4,128)}, u32[]{:S(2)}) copy-start(f32[3,9,9,128]{3,0,2,1:T(4,128)} %param.15) | copy-start | bytes 373252
  5.3 0.9 %copy-start.4 = (f32[4,35,35]{2,0,1:T(4,128)S(1)}, f32[4,35,35]{2,0,1:T(4,128)}, u32[]{:S(2)}) copy-start(f32[4,35,35]{2,0,1:T(4,128)} %param.18) | copy-start | bytes 58804
  6.2 0.8 %copy-start.5 = (f32[3,35,35]{2,1,0:T(8,128)S(1)}, f32[3,35,35]{2,1,0:T(8,128)}, u32[]{:S(2)}) copy-start(f32[3,35,35]{2,1,0:T(8,128)} %stiff_in.1) | copy-start | bytes 44104

commit v2 on v1

--- a/solution.py
+++ b/solution.py
@@ -163,7 +163,7 @@
     )
 
     def min_copy(stage, slot, off):
-        axis = ("depth", "strike")[stage % 2]
+        axis = ("strike", "depth")[stage % 2]
         me, count = groups[axis]
         return pltpu.make_async_remote_copy(
             src_ref=minima.at[stage, slot],
@@ -175,17 +175,17 @@
         )
 
     def min_offsets(stage):
-        count = groups[("depth", "strike")[stage % 2]][1]
+        count = groups[("strike", "depth")[stage % 2]][1]
         return [off for off in order if off < count]
 
     def min_start(stage, row):
-        me, count = groups[("depth", "strike")[stage % 2]]
+        me, count = groups[("strike", "depth")[stage % 2]]
         minima[stage, me] = row
         for off in min_offsets(stage):
             min_copy(stage, me, off).start()
 
     def min_finish(stage):
-        me, count = groups[("depth", "strike")[stage % 2]]
+        me, count = groups[("strike", "depth")[stage % 2]]
         for off in reversed(min_offsets(stage)):
             min_copy(stage, lax.rem(me + off, count), off).wait_recv()
         rows = [minima[stage, other] for other in range(count)]
@@ -194,7 +194,7 @@
         return rows[0]
 
     def min_drain(stage):
-        me, _ = groups[("depth", "strike")[stage % 2]]
+        me, _ = groups[("strike", "depth")[stage % 2]]
         for off in min_offsets(stage):
             min_copy(stage, me, off).wait_send()
 
@@ -305,6 +305,10 @@
                     sums[q] = sums[q] + weight(q, p, g) * field
             return tuple(sums)
 
+        if rows <= 16:
+            for p in range(Q):
+                sums = body(p, sums)
+            return sums
         return lax.fori_loop(0, Q, body, tuple(sums))
 
     def nothing(rows):
@@ -347,13 +351,6 @@
         sent_a[1, q, 24:32, :] = series_2[q, 0:8]
         sent_a[1, q, 32:40, :] = series_2[q, 8:16] + pltpu.roll(series_4[q], 2, 0)
 
-    loads[7].wait()
-    pl.semaphore_wait(barrier, n_depth + n_strike - 2)
-    min_start(0, own_ratio)
-    to_all(lambda k, where: side_copy(k, where).start())
-    for piece in range(2):
-        to_all(lambda k, where: halo_copy(piece, k, where).start())
-
     loads[8].wait()
 
     def pack(q, carry):
@@ -399,12 +396,15 @@
             part[k, q] = sums[q]
 
     own_fine(0)
-    own_fine(1)
-    own_fine(2)
-    row = min_finish(0)
-    min_start(1, row)
-    own_fine(3)
-    own_fine(4)
+    loads[7].wait()
+    pl.semaphore_wait(barrier, n_depth + n_strike - 2)
+    min_start(0, own_ratio)
+    to_all(lambda k, where: side_copy(k, where).start())
+    for piece in range(2):
+        to_all(lambda k, where: halo_copy(piece, k, where).start())
+
+    for k in range(1, 5):
+        own_fine(k)
 
     def paired(ref):
         rows = [ref[f : f + 1, :] for f in range(4)]
@@ -414,6 +414,26 @@
             jnp.where(left_row, swap(rows[0]), rows[1]),
             jnp.where(left_row, swap(rows[2]), rows[3]),
         ]
+
+    loads[12].wait()
+    place = lax.broadcasted_iota(jnp.int32, (E, E), 0)
+
+    def one_hot(mask):
+        return jnp.where(mask, 1.0, 0.0).astype(bf16)
+
+    sources = paired(source)
+    from_all(lambda k, where: side_copy(k, where).wait_recv())
+    for k in range(5):
+        right = jnp.concatenate([one_hot(place == row - (E + k * E) % (5 * E)) for row in sources], axis=1)
+        if k < 4:
+            row = ROW_OF_SLOT[k]
+            left = one_hot(place == side_got[k, row : row + 1, :])
+            right = jnp.dot(left, right, preferred_element_type=f32).astype(bf16)
+        pick[k, 0:E, :] = right
+        pick[k, E : 2 * E, :] = right
+
+    row = min_finish(0)
+    min_start(1, row)
 
     loads[11].wait()
     number = lax.rem(lax.broadcasted_iota(jnp.int32, (E, E), 0), NSEL)
@@ -450,42 +470,26 @@
 
     lax.fori_loop(0, 7, choose, 0)
 
-    loads[12].wait()
-    place = lax.broadcasted_iota(jnp.int32, (E, E), 0)
-
-    def one_hot(mask):
-        return jnp.where(mask, 1.0, 0.0).astype(bf16)
-
-    sources = paired(source)
-    from_all(lambda k, where: side_copy(k, where).wait_recv())
-    for k in range(5):
-        right = jnp.concatenate([one_hot(place == row - (E + k * E) % (5 * E)) for row in sources], axis=1)
-        if k < 4:
-            row = ROW_OF_SLOT[k]
-            left = one_hot(place == side_got[k, row : row + 1, :])
-            right = jnp.dot(left, right, preferred_element_type=f32).astype(bf16)
-        pick[k, 0:E, :] = right
-        pick[k, E : 2 * E, :] = right
-
-    def gather(blocks):
+    def gather(blocks, columns):
         total = None
         for k in range(5):
             high, low = split(blocks[k])
             left = jnp.concatenate([high, low], axis=1)
-            value = jnp.dot(left, pick[k], preferred_element_type=f32)
+            value = jnp.dot(left, pick[k, :, columns], preferred_element_type=f32)
             total = value if total is None else total + value
         return total
 
-    for piece in range(2):
-        from_all(lambda k, where: halo_copy(piece, k, where).wait_recv())
+    def gather_series(piece, half):
         for chunk in range(3):
             rows = slice(3 * chunk, 3 * chunk + 3)
             total = gather(
                 [got_a[k, piece, rows].reshape(3 * BP, E) for k in range(4)]
-                + [sent_a[piece, rows].reshape(3 * BP, E)]
+                + [sent_a[piece, rows].reshape(3 * BP, E)],
+                slice(2 * half * E, 2 * half * E + 2 * E),
             )
-            for g in range(4):
-                gathered[piece, g, chunk * 3 * BP : (chunk + 1) * 3 * BP, :] = total[:, g * E : (g + 1) * E]
+            for g in range(2):
+                place = slice(chunk * 3 * BP, (chunk + 1) * 3 * BP)
+                gathered[piece, 2 * half + g, place, :] = total[:, g * E : (g + 1) * E]
 
     def near(source_row, count, g, row):
         sums = nothing(BP)
@@ -498,15 +502,15 @@
 
     for k in range(5):
         block, start, count = TERMS[k]
-
-        def face(g, carry, block=block, start=start, count=count):
-            near(lambda p, j: gathered[block, g, pl.ds(p * BP + start + j, 1), :], count, g, 4 + g)
+        if k < 2:
+            from_all(lambda k, where: halo_copy(block, k, where).wait_recv())
+            gather_series(block, 0)
+
+        def face(g, carry, k=k, block=block, start=start, count=count):
+            near(lambda p, j: gathered[block, g, pl.ds(p * BP + start + j, 1), :], count, g, 2 * k + g)
             return carry
 
         lax.fori_loop(0, 2, face, 0)
-        sums = contract(fine_weight(0), range(4, 6), BP, [part[k, q] for q in range(Q)])
-        for q in range(Q):
-            part[k, q] = sums[q]
 
     step = jnp.min(min_finish(1), axis=1, keepdims=True) * COURANT
     step = jnp.broadcast_to(step, (1, E))
@@ -528,10 +532,21 @@
     for q in range(Q):
         first[q] = taylor(sent_a.at[0], q, powers)
         second[q] = taylor(sent_a.at[0], q, late)
-        change = powers[0] * part[0, q]
+    for p in range(Q):
+        for g in range(2):
+            value = powers[0] * applied[g, p]
+            for k in range(1, 5):
+                value = value + powers[k] * applied[2 * k + g, p]
+            applied[g, p] = value
+    changes = []
+    for q in range(Q):
+        value = powers[0] * part[0, q]
         for k in range(1, 5):
-            change = change + powers[k] * part[k, q]
-        change = change + swap(change)
+            value = value + powers[k] * part[k, q]
+        changes.append(value)
+    changes = contract(fine_weight(4), range(2), BP, changes)
+    for q in range(Q):
+        change = changes[q] + swap(changes[q])
         middle[q] = twice(sent_a[0, q]) + scaled(q, change, gain_fine)
     for index in range(4):
         base = middle if index == 0 else series[index]
@@ -539,7 +554,6 @@
     fine_left = jnp.logical_and(fine, left_row)
     for q in range(Q):
         applied[10, q] = taylor(middle, q, powers)
-    for q in range(Q):
         second[q] = jnp.where(fine_left, applied[10, q], second[q])
 
     energy = jnp.zeros((1, E), f32)
@@ -573,6 +587,9 @@
     for q in range(Q):
         base = jnp.where(fine_left, middle[q], sent_a[0, q])
         middle[q] = base
+
+    for piece in range(2):
+        gather_series(piece, 1)
 
     coarse_halves = [
         jnp.where(left_row, coarse, swap(coarse)),
@@ -603,7 +620,7 @@
     from_all(lambda k, where: halo_copy(2, k, where).wait_recv())
     for n in range(5):
         blocks = [got_b[k, n] for k in range(4)] + [sent_b[n]]
-        total = gather([jnp.concatenate([x, swap(x)], axis=0) for x in blocks])
+        total = gather([jnp.concatenate([x, swap(x)], axis=0) for x in blocks], slice(0, 4 * E))
         for half in range(2 if n < 4 else 1):
             rows = slice((2 * n + half) * BP, (2 * n + half + 1) * BP)
             for g in range(4):
@@ -656,16 +673,17 @@
     wave_speed,
     damage_rate,
 ):
+    out_shape = (
+        jax.ShapeDtypeStruct((Q, B, E), f32),
+        jax.ShapeDtypeStruct((1, E), f32),
+        jax.ShapeDtypeStruct((1, 1), f32),
+    )
     most = max(n_strike, n_depth)
     vmem = pltpu.VMEM
     dma = pltpu.SemaphoreType.DMA
     call = pl.pallas_call(
         functools.partial(kernel, n_strike, n_depth),
-        out_shape=(
-            jax.ShapeDtypeStruct((Q, B, E), f32),
-            jax.ShapeDtypeStruct((1, E), f32),
-            jax.ShapeDtypeStruct((1, 1), f32),
-        ),
+        out_shape=out_shape,
         in_specs=[pl.BlockSpec(memory_space=pltpu.HBM)] * 14,
         out_specs=tuple(pl.BlockSpec(memory_space=pltpu.VMEM) for _ in range(3)),
         scratch_shapes=[
@@ -723,7 +741,7 @@
         ),
     )
     row = (1, E)
-    final, new_damage, next_step = call(
+    operands = (
         dof_values,
         jnp.transpose(star_matrices, (1, 2, 0, 3)),
         jnp.transpose(flux_solvers, (0, 2, 3, 1, 4)),
@@ -738,6 +756,9 @@
         element_size.reshape(row),
         wave_speed.reshape(row),
         damage_rate.reshape(row),
+    )
+    final, new_damage, next_step = call(
+        *(pltpu.with_memory_space_constraint(x, pltpu.HBM) for x in operands)
     )
     return final, new_damage.reshape(E), next_step.reshape(())
 

time: 48.4 us -> 41.7 us (0.86)
  local copies, waits for them, and re-layouts: 7.52 us -> 1.19 us
    unnamed x30 -> x2, local copies, waits for them, and re-layouts: 7.52 us -> 1.19 us
where the time goes in v2:
time: 41.7 us; the launch traced here: 41.6 us
  Pallas kernels  38.1 us (91%)
  between operations  2.33 us (6%)
  local copies, waits for them, and re-layouts  1.19 us (3%)
    pallas_call x1, Pallas kernels, shards(): call(*(pltpu.with_memory_space_constraint(x, pltpu.HBM) for x in operands))  38.1 us
    unnamed x2, local copies, waits for them, and re-layouts  1.19 us

profile of v2, /device:TPU:1, one launch (start us, length us, event | category | flops | bytes accessed | tf_op | source)
XLA Modules:
  0.0 41.6 jit_solution(17868287309002314939)
XLA Ops:
  0.6 38.1 %shard_map.157 = (f32[9,35,128]{2,1,0:T(8,128)S(1)}, f32[1,128]{1,0:T(1,128)S(1)}, f32[1,1]{1,0:T(1,128)}) custom-call(f32[9,35,128]{2,1,0:T(8,128)} %dof_in.1, f32[9,9,3,128]{3,2,1,0:T(4,128)} %bitcast.14, f32[2,9,9,4,128]{4,3,2,1,0:T(4,128)} %bitcast.13, f32[3,35,35]{2,1,0:T(8,128)} %stiff_in.1, f32[35,4,35]{2,1,0:T(4,128)} %bitcast.15, ...), custom_call_target="tpu_custom_call" | custom-call | tf_op jit(solution)/shard_map/pallas_call | solution.py:760
  38.7 0.7 %copy.20 = f32[9,35,128]{2,1,0:T(8,128)} copy(f32[9,35,128]{2,1,0:T(8,128)S(1)} %get-tuple-element.12) | data formatting | bytes 322560
  39.4 0.5 %copy.21 = f32[128]{0:T(128)} copy(f32[128]{0:T(128)S(1)} %bitcast.11) | data formatting | bytes 1024

commit v3 on v2

--- a/solution.py
+++ b/solution.py
@@ -17,8 +17,13 @@
 MESH = pl.DeviceIdType.MESH
 f32, bf16 = jnp.float32, jnp.bfloat16
 ROW_OF_SLOT = (1, 0, 3, 2)
-TERMS = ((0, 0, 35), (1, 0, 20), (1, 24, 10), (1, 20, 4), (1, 34, 1))
-MARK = 35
+START, HEIGHT = (0, 32), (32, 40)
+SENT = 72
+MARK = 38
+CHUNKS = 1
+PER = Q // CHUNKS
+STAGES = ("strike", "depth", "depth", "strike")
+LAST = ((0, 5),)
 ROWS = (40, 24, 16, 8, 8)
 SLOTS = (48, 32, 16, 16, 16)
 
@@ -84,9 +89,10 @@
     rate,
     minima,
     side_got,
-    sent_a,
+    dof,
+    sent,
     sent_b,
-    got_a,
+    got,
     got_b,
     series_1,
     series_2,
@@ -104,10 +110,12 @@
     matrix_2,
     matrix_u,
     applied,
+    face_terms,
     part,
     chosen,
     pick,
-    gathered,
+    gathered_0,
+    gathered_1,
     remote,
     load_sem,
     min_send,
@@ -118,7 +126,8 @@
     halo_recv,
 ):
     s, d = lax.axis_index("strike"), lax.axis_index("depth")
-    series = (sent_a.at[0], series_1, series_2, series_3, series_4)
+    gathered = (gathered_0, gathered_1)
+    series = (dof, series_1, series_2, series_3, series_4)
 
     loads = [
         pltpu.make_async_copy(src, dst, load_sem.at[index])
@@ -128,10 +137,10 @@
                 (size_in, size),
                 (speed_in, speed),
                 (dof_in, dof_raw),
-                (cluster_in, cluster),
+                (side_in, side),
                 (stiff_in, wide_stiff),
                 (star_in, star),
-                (side_in, side),
+                (cluster_in, cluster),
                 (solver_in, solver),
                 (local_in, wide_local),
                 (flat_in, wide_flat),
@@ -163,7 +172,7 @@
     )
 
     def min_copy(stage, slot, off):
-        axis = ("strike", "depth")[stage % 2]
+        axis = STAGES[stage]
         me, count = groups[axis]
         return pltpu.make_async_remote_copy(
             src_ref=minima.at[stage, slot],
@@ -175,17 +184,17 @@
         )
 
     def min_offsets(stage):
-        count = groups[("strike", "depth")[stage % 2]][1]
+        count = groups[STAGES[stage]][1]
         return [off for off in order if off < count]
 
     def min_start(stage, row):
-        me, count = groups[("strike", "depth")[stage % 2]]
+        me, count = groups[STAGES[stage]]
         minima[stage, me] = row
         for off in min_offsets(stage):
             min_copy(stage, me, off).start()
 
     def min_finish(stage):
-        me, count = groups[("strike", "depth")[stage % 2]]
+        me, count = groups[STAGES[stage]]
         for off in reversed(min_offsets(stage)):
             min_copy(stage, lax.rem(me + off, count), off).wait_recv()
         rows = [minima[stage, other] for other in range(count)]
@@ -194,16 +203,23 @@
         return rows[0]
 
     def min_drain(stage):
-        me, _ = groups[("strike", "depth")[stage % 2]]
+        me, _ = groups[STAGES[stage]]
         for off in min_offsets(stage):
             min_copy(stage, me, off).wait_send()
 
-    def halo_copy(piece, k, where):
+    def halo_copy(piece, chunk, k, where):
+        if piece < 2:
+            rows = pl.ds(chunk * PER, PER)
+            height = pl.ds(START[piece], HEIGHT[piece])
+            src, dst = sent.at[rows, height], got.at[k, rows, height]
+        else:
+            rows = pl.ds(LAST[chunk][0], LAST[chunk][1] - LAST[chunk][0])
+            src, dst = sent_b.at[rows], got_b.at[k, rows]
         return pltpu.make_async_remote_copy(
-            src_ref=sent_a.at[piece] if piece < 2 else sent_b,
-            dst_ref=got_a.at[k, piece] if piece < 2 else got_b.at[k],
-            send_sem=halo_send.at[piece, k],
-            recv_sem=halo_recv.at[piece, k],
+            src_ref=src,
+            dst_ref=dst,
+            send_sem=halo_send.at[piece, chunk, k],
+            recv_sem=halo_recv.at[piece, chunk, k],
             device_id=where,
             device_id_type=MESH,
         )
@@ -218,8 +234,8 @@
             device_id_type=MESH,
         )
 
-    def to_all(send):
-        for k in range(4):
+    def to_all(send, ks=range(4)):
+        for k in ks:
             exists, where = towards[k]
 
             @pl.when(exists)
@@ -232,18 +248,6 @@
             @pl.when(has[k])
             def _(k=k):
                 receive(k, towards[k][1])
-
-    for k in range(4):
-
-        @pl.when(jnp.logical_not(has[k]))
-        def _(k=k):
-            got_a[k] = jnp.zeros((2, Q, BP, E), f32)
-            got_b[k] = jnp.zeros((5, BP, E), f32)
-            side_got[k] = jnp.full((4, E), -1, jnp.int32)
-
-    stack[96:128, :] = jnp.zeros((32, Q * E), bf16)
-    stack[176:256, :] = jnp.zeros((80, Q * E), bf16)
-    stiff[...] = jnp.zeros((7, E, E), f32)
 
     left_half = lax.broadcasted_iota(jnp.int32, (BP, E), 1) < HALF
     left_row = left_half[0:1]
@@ -260,14 +264,34 @@
         load.wait()
     gain = 1.0 - damage[...]
     own_ratio = size[...] / (speed[...] * jnp.sqrt(gain))
-
+    pl.semaphore_wait(barrier, n_depth + n_strike - 2)
+    min_start(0, own_ratio)
     loads[3].wait()
+    for q in range(Q):
+        sent[q, 0:32, :] = dof_raw[q, 0:32, :]
+    for ks in ((0, 1), (2, 3)):
+        for chunk in range(CHUNKS):
+            to_all(lambda k, where: halo_copy(0, chunk, k, where).start(), ks)
     loads[4].wait()
+    to_all(lambda k, where: side_copy(k, where).start())
+
+    for k in range(4):
+
+        @pl.when(jnp.logical_not(has[k]))
+        def _(k=k):
+            got[k] = jnp.zeros((Q, SENT, E), f32)
+            got_b[k] = jnp.zeros((5, BP, E), f32)
+            side_got[k] = jnp.full((4, E), -1, jnp.int32)
+
+    stack[96:128, :] = jnp.zeros((32, Q * E), bf16)
+    stack[176:256, :] = jnp.zeros((80, Q * E), bf16)
+    stiff[...] = jnp.zeros((7, E, E), f32)
+
+    loads[7].wait()
     coarse = jnp.where(cluster[...] != 0, 1.0, 0.0)
     for q in range(Q):
-        sent_a[0, q, 32:BP, :] = jnp.zeros((8, E), f32)
-        sent_a[0, q, 0:B, :] = dof_raw[q]
-    sent_a[0, 0, MARK : MARK + 1, :] = coarse
+        dof[q, 32:BP, :] = jnp.zeros((8, E), f32)
+        dof[q, 0:B, :] = dof_raw[q]
 
     loads[5].wait()
     inside = jnp.logical_and(sub < B, lane < B)
@@ -320,8 +344,14 @@
     def star_weight(q, p, c):
         return star[q, p, c : c + 1, :]
 
+    pack_rows = (16, 18, 0, 2, 4, 6, 12, 14)
+
     def fine_weight(shift):
-        return lambda q, p, g: fine_weights[q, p, g + shift : g + shift + 1, :]
+        def weight(q, p, g):
+            row = pack_rows[g + shift]
+            return fine_weights[q, p, row : row + 1, :]
+
+        return weight
 
     def derive(source_rows, order_in, target, fine):
         matrix = (matrix_0, matrix_1, matrix_2, matrix_2)[order_in]
@@ -345,31 +375,34 @@
     loads[6].wait()
     for index in range(4):
         derive(lambda p, index=index: series[index][p], index, series[index + 1], False)
-    for q in range(Q):
-        sent_a[1, q, 0:16, :] = series_1[q, 0:16]
-        sent_a[1, q, 16:24, :] = series_1[q, 16:24] + pltpu.roll(series_3[q], 4, 0)
-        sent_a[1, q, 24:32, :] = series_2[q, 0:8]
-        sent_a[1, q, 32:40, :] = series_2[q, 8:16] + pltpu.roll(series_4[q], 2, 0)
+    sub8 = lax.broadcasted_iota(jnp.int32, (8, E), 0)
+    for q in range(Q):
+        turned = pltpu.roll(series_2[q, 0:8], 4, 0)
+        sent[q, 32:40, :] = (
+            dof[q, 32:BP, :] + pltpu.roll(series_3[q], 3, 0) + pltpu.roll(series_4[q], 7, 0)
+        )
+        sent[q, 40:56, :] = series_1[q, 0:16]
+        sent[q, 56:64, :] = series_1[q, 16:24] + jnp.where(sub8 >= 4, turned, 0.0)
+        sent[q, 64:72, :] = jnp.where(sub8 < 4, turned, 0.0) + pltpu.roll(series_2[q, 8:16], 4, 0)
+    sent[0, 32 + MARK : 33 + MARK, :] = coarse
+    for ks in ((0, 1), (2, 3)):
+        for chunk in range(CHUNKS):
+            to_all(lambda k, where: halo_copy(1, chunk, k, where).start(), ks)
 
     loads[8].wait()
+
+    left8 = left_half[0:8]
+    row8 = lax.broadcasted_iota(jnp.int32, (8, E), 0)
 
     def pack(q, carry):
         for p in range(Q):
-            rows = [star[q, p, c : c + 1, :] for c in range(3)]
-            own = [solver[0, q, p, f : f + 1, :] for f in range(4)]
-            other = [solver[1, q, p, f : f + 1, :] for f in range(4)]
-            tile = [
-                jnp.where(left_row, rows[0], swap(rows[1])),
-                jnp.where(left_row, rows[2], 0.0),
-                jnp.where(left_row, own[0], swap(own[1])),
-                jnp.where(left_row, own[2], swap(own[3])),
-                jnp.where(left_row, other[0], swap(other[1])),
-                jnp.where(left_row, other[2], swap(other[3])),
-                jnp.where(left_row, swap(other[0]), other[1]),
-                jnp.where(left_row, swap(other[2]), other[3]),
-            ]
-            for r in range(8):
-                fine_weights[q, p, r : r + 1, :] = tile[r]
+            both = jnp.concatenate([solver[0, q, p], solver[1, q, p]], axis=0)
+            turned = swap(both)
+            fine_weights[q, p, 0:8, :] = jnp.where(left8, both, pltpu.roll(turned, 7, 0))
+            fine_weights[q, p, 8:16, :] = jnp.where(left8, turned, pltpu.roll(both, 7, 0))
+            ways = jnp.concatenate([star[q, p], jnp.zeros((5, E), f32)], axis=0)
+            other = jnp.where(row8 == 0, pltpu.roll(swap(ways), 7, 0), 0.0)
+            fine_weights[q, p, 16:24, :] = jnp.where(left8, ways, other)
         return carry
 
     lax.fori_loop(0, Q, pack, 0)
@@ -382,29 +415,15 @@
         stiff[3 + f, 0:B, 0:B] = wide_local[:, f, :]
         matrix_u[(3 + f) * BP : (4 + f) * BP, :] = -stiff[3 + f, 0:BP, :]
 
-    def own_fine(k):
-        put_stack(lambda p: twice(series[k][p]), SLOTS[k])
-        product = stacked_dot(make_stack(matrix_u[...], SLOTS[k]), SLOTS[k])
+    def own_fine():
+        put_stack(lambda p: twice(first[p]), 48)
+        product = stacked_dot(make_stack(matrix_u[...], 48), 48)
         for p in range(Q):
             pieces = [product[g * BP : (g + 1) * BP, p * E : (p + 1) * E] for g in range(7)]
             applied[0, p] = jnp.where(left_half, pieces[0], pieces[1])
             applied[1, p] = pieces[2]
             applied[2, p] = jnp.where(left_half, pieces[3], pieces[4])
             applied[3, p] = jnp.where(left_half, pieces[5], pieces[6])
-        sums = contract(fine_weight(0), range(4), BP, nothing(BP))
-        for q in range(Q):
-            part[k, q] = sums[q]
-
-    own_fine(0)
-    loads[7].wait()
-    pl.semaphore_wait(barrier, n_depth + n_strike - 2)
-    min_start(0, own_ratio)
-    to_all(lambda k, where: side_copy(k, where).start())
-    for piece in range(2):
-        to_all(lambda k, where: halo_copy(piece, k, where).start())
-
-    for k in range(1, 5):
-        own_fine(k)
 
     def paired(ref):
         rows = [ref[f : f + 1, :] for f in range(4)]
@@ -422,95 +441,88 @@
         return jnp.where(mask, 1.0, 0.0).astype(bf16)
 
     sources = paired(source)
-    from_all(lambda k, where: side_copy(k, where).wait_recv())
-    for k in range(5):
-        right = jnp.concatenate([one_hot(place == row - (E + k * E) % (5 * E)) for row in sources], axis=1)
-        if k < 4:
+
+    def point():
+        for k in range(4):
+            right = jnp.concatenate([one_hot(place == row - (E + k * E)) for row in sources], axis=1)
             row = ROW_OF_SLOT[k]
             left = one_hot(place == side_got[k, row : row + 1, :])
             right = jnp.dot(left, right, preferred_element_type=f32).astype(bf16)
-        pick[k, 0:E, :] = right
-        pick[k, E : 2 * E, :] = right
-
+            pick[k, 0:E, :] = right
+            pick[k, E : 2 * E, :] = right
+
+    from_all(lambda k, where: side_copy(k, where).wait_recv())
+    point()
     row = min_finish(0)
     min_start(1, row)
 
     loads[11].wait()
+    selects = paired(select)
+    loads[10].wait()
+    flat[...] = jnp.zeros((B * BP, E), f32)
+    for i in range(B):
+        flat[pl.ds(i, B, stride=BP), 0:NSEL] = wide_flat[i]
     number = lax.rem(lax.broadcasted_iota(jnp.int32, (E, E), 0), NSEL)
     usable = lax.broadcasted_iota(jnp.int32, (E, E), 0) < 2 * NSEL
     hot = jnp.concatenate(
         [
             jnp.where(jnp.logical_and(number == row, usable), -1.0, 0.0).astype(bf16)
-            for row in paired(select)
+            for row in selects
         ],
         axis=1,
     )
-    loads[10].wait()
-    flat[...] = jnp.zeros((B * BP, E), f32)
-
-    def clear(j, carry):
-        for g in range(4):
-            chosen[g, pl.ds(pl.multiple_of(j * BP + 32, 8), 8), :] = jnp.zeros((8, E), f32)
-        return carry
-
-    lax.fori_loop(0, B, clear, 0)
 
     def choose(index, carry):
-        for n in range(5):
-            flat[pl.ds(pl.multiple_of((index * 5 + n) * BP, 8), B), 0:NSEL] = wide_flat[index * 5 + n]
-        high, low = split(flat[pl.ds(pl.multiple_of(index * 200, 8), 200), :])
+        rows = pl.ds(pl.multiple_of(index * 200, 8), 200)
+        high, low = split(flat[rows, :])
         left = (high.astype(f32) + pltpu.roll(low.astype(f32), NSEL, 1)).astype(bf16)
         product = jnp.dot(left, hot, preferred_element_type=f32)
-        for n in range(5):
-            for g in range(4):
-                chosen[g, pl.ds(index * 5 + n, B, stride=BP), :] = product[
-                    n * BP : n * BP + B, g * E : (g + 1) * E
-                ]
+        for g in range(4):
+            chosen[g, rows, :] = product[:, g * E : (g + 1) * E]
         return carry
 
     lax.fori_loop(0, 7, choose, 0)
 
-    def gather(blocks, columns):
+    def gather(blocks):
         total = None
-        for k in range(5):
+        for k in range(4):
             high, low = split(blocks[k])
             left = jnp.concatenate([high, low], axis=1)
-            value = jnp.dot(left, pick[k, :, columns], preferred_element_type=f32)
+            value = jnp.dot(left, pick[k], preferred_element_type=f32)
             total = value if total is None else total + value
         return total
 
-    def gather_series(piece, half):
-        for chunk in range(3):
-            rows = slice(3 * chunk, 3 * chunk + 3)
+    def gather_series(piece):
+        height = HEIGHT[piece]
+        for part_of in range(3):
+            rows = slice(part_of * 3, part_of * 3 + 3)
             total = gather(
-                [got_a[k, piece, rows].reshape(3 * BP, E) for k in range(4)]
-                + [sent_a[piece, rows].reshape(3 * BP, E)],
-                slice(2 * half * E, 2 * half * E + 2 * E),
+                [got[k, rows, START[piece] : START[piece] + height].reshape(3 * height, E) for k in range(4)]
             )
-            for g in range(2):
-                place = slice(chunk * 3 * BP, (chunk + 1) * 3 * BP)
-                gathered[piece, 2 * half + g, place, :] = total[:, g * E : (g + 1) * E]
-
-    def near(source_row, count, g, row):
-        sums = nothing(BP)
+            for g in range(4):
+                where = slice(part_of * 3 * height, (part_of + 1) * 3 * height)
+                gathered[piece][g, where, :] = total[:, g * E : (g + 1) * E]
+
+    def near(source_row, first_j, count, g, ps, sums):
         for j in range(count):
-            matrix = chosen[g, j * BP : (j + 1) * BP, :]
-            for p in range(Q):
-                sums[p] = sums[p] + matrix * source_row(p, j)
+            matrix = chosen[g, (first_j + j) * BP : (first_j + j + 1) * BP, :]
+            for n, p in enumerate(ps):
+                sums[n] = sums[n] + matrix * source_row(p, j)
+        return sums
+
+    for chunk in range(CHUNKS):
+        from_all(lambda k, where: halo_copy(0, chunk, k, where).wait_recv())
+
+    gather_series(0)
+
+    def face_before(g, carry):
+        sums = [jnp.zeros((BP, E), f32) for _ in range(Q)]
+        sums = near(lambda p, j: gathered_0[g, p * 32 + j : p * 32 + j + 1, :], 0, 32, g, range(Q), sums)
         for p in range(Q):
-            applied[row, p] = sums[p]
-
-    for k in range(5):
-        block, start, count = TERMS[k]
-        if k < 2:
-            from_all(lambda k, where: halo_copy(block, k, where).wait_recv())
-            gather_series(block, 0)
-
-        def face(g, carry, k=k, block=block, start=start, count=count):
-            near(lambda p, j: gathered[block, g, pl.ds(p * BP + start + j, 1), :], count, g, 2 * k + g)
-            return carry
-
-        lax.fori_loop(0, 2, face, 0)
+            face_terms[g, p] = sums[p]
+        return carry
+
+    lax.fori_loop(0, 2, face_before, 0)
 
     step = jnp.min(min_finish(1), axis=1, keepdims=True) * COURANT
     step = jnp.broadcast_to(step, (1, E))
@@ -530,24 +542,57 @@
 
     fine = coarse < 0.5
     for q in range(Q):
-        first[q] = taylor(sent_a.at[0], q, powers)
-        second[q] = taylor(sent_a.at[0], q, late)
-    for p in range(Q):
+        first[q] = taylor(dof, q, powers)
+        second[q] = taylor(dof, q, late)
+    own_fine()
+    changes = contract(fine_weight(0), range(4), BP, nothing(BP))
+    for q in range(Q):
+        part[0, q] = changes[q]
+
+    def series_tiles(g, p):
+        mixed = gathered_1[g, p * 40 : p * 40 + 8, :]
+        high = [gathered_1[g, p * 40 + 8 * t : p * 40 + 8 * t + 8, :] for t in range(1, 5)]
+        turned = pltpu.roll(high[3], 4, 0)
+        d_1 = (high[0], high[1], jnp.where(sub8 < 4, high[2], 0.0))
+        d_2 = (
+            jnp.where(sub8 < 4, pltpu.roll(high[2], 4, 0), turned),
+            jnp.where(sub8 < 2, turned, 0.0),
+        )
+        d_3 = jnp.where(sub8 < 4, pltpu.roll(mixed, 5, 0), 0.0)
+        d_4 = jnp.where(sub8 < 1, pltpu.roll(mixed, 1, 0), 0.0)
+        return mixed, d_1, d_2, d_3, d_4
+
+    def summed_tiles(tiles, weight):
+        mixed, d_1, d_2, d_3, d_4 = tiles
+        return (
+            weight[1] * d_1[0] + weight[2] * d_2[0] + weight[3] * d_3 + weight[4] * d_4,
+            weight[1] * d_1[1] + weight[2] * d_2[1],
+            weight[1] * d_1[2],
+            weight[0] * mixed,
+        )
+
+    for chunk in range(CHUNKS):
+        ps = range(chunk * PER, (chunk + 1) * PER)
+        from_all(lambda k, where: halo_copy(1, chunk, k, where).wait_recv())
+        gather_series(1)
         for g in range(2):
-            value = powers[0] * applied[g, p]
-            for k in range(1, 5):
-                value = value + powers[k] * applied[2 * k + g, p]
-            applied[g, p] = value
-    changes = []
-    for q in range(Q):
-        value = powers[0] * part[0, q]
-        for k in range(1, 5):
-            value = value + powers[k] * part[k, q]
-        changes.append(value)
-    changes = contract(fine_weight(4), range(2), BP, changes)
+            for p in ps:
+                for t, tile in enumerate(summed_tiles(series_tiles(g, p), powers)):
+                    remote[g, p * BP + 8 * t : p * BP + 8 * t + 8, :] = tile
+
+        def face_after(g, carry, ps=ps):
+            sums = [powers[0] * face_terms[g, p] for p in ps]
+            sums = near(lambda p, j: remote[g, p * BP + j : p * BP + j + 1, :], 0, 20, g, ps, sums)
+            sums = near(lambda p, j: remote[g, p * BP + 24 + j : p * BP + 25 + j, :], 32, 3, g, ps, sums)
+            for n, p in enumerate(ps):
+                applied[4 + g, p] = sums[n]
+            return carry
+
+        lax.fori_loop(0, 2, face_after, 0)
+    changes = contract(fine_weight(0), range(4, 6), BP, [part[0, q] for q in range(Q)])
     for q in range(Q):
         change = changes[q] + swap(changes[q])
-        middle[q] = twice(sent_a[0, q]) + scaled(q, change, gain_fine)
+        middle[q] = twice(dof[q]) + scaled(q, change, gain_fine)
     for index in range(4):
         base = middle if index == 0 else series[index]
         derive(lambda p, base=base: base[p], index, series[index + 1], True)
@@ -570,7 +615,8 @@
     for n in range(5):
         other = applied[10, 2 * n + 1] if n < 4 else jnp.zeros((BP, E), f32)
         sent_b[n] = jnp.where(left_half, applied[10, 2 * n], other) * fine_both
-    to_all(lambda k, where: halo_copy(2, k, where).start())
+    for chunk in range(CHUNKS):
+        to_all(lambda k, where: halo_copy(2, chunk, k, where).start())
 
     put_stack(lambda p: second[p] + coarse * first[p], 48)
     product = stacked_dot(make_stack(matrix_u[...], 48), 48)
@@ -585,53 +631,50 @@
     for q in range(Q):
         part[0, q] = sums[q]
     for q in range(Q):
-        base = jnp.where(fine_left, middle[q], sent_a[0, q])
+        base = jnp.where(fine_left, middle[q], dof[q])
         middle[q] = base
 
-    for piece in range(2):
-        gather_series(piece, 1)
+    row = min_finish(2)
+    min_start(3, row)
 
     coarse_halves = [
         jnp.where(left_row, coarse, swap(coarse)),
         jnp.where(left_row, swap(coarse), coarse),
     ]
-    sub8 = lax.broadcasted_iota(jnp.int32, (8, E), 0)
     for g in range(4):
-        theirs = gathered[0, g, MARK : MARK + 1, :]
+        theirs = gathered_1[g, MARK : MARK + 1, :]
         weight = [late[k] * theirs + powers[k] * coarse_halves[g // 2] for k in range(5)]
         for p in range(Q):
-            low = [gathered[0, g, p * BP + 8 * t : p * BP + 8 * t + 8, :] for t in range(5)]
-            high = [gathered[1, g, p * BP + 8 * t : p * BP + 8 * t + 8, :] for t in range(5)]
-            value = [weight[0] * x for x in low]
-            d_3 = jnp.where(sub8 < 4, pltpu.roll(high[2], 4, 0), 0.0)
-            d_4 = jnp.where(sub8 < 1, pltpu.roll(high[4], 6, 0), 0.0)
-            value[0] = value[0] + weight[1] * high[0] + weight[2] * high[3] + weight[3] * d_3 + weight[4] * d_4
-            value[1] = value[1] + weight[1] * high[1] + weight[2] * jnp.where(sub8 < 2, high[4], 0.0)
-            value[2] = value[2] + weight[1] * jnp.where(sub8 < 4, high[2], 0.0)
+            tiles = summed_tiles(series_tiles(g, p), weight)
+            value = [weight[0] * gathered_0[g, p * 32 + 8 * t : p * 32 + 8 * t + 8, :] for t in range(4)]
+            value = [value[0] + tiles[0], value[1] + tiles[1], value[2] + tiles[2], value[3], tiles[3]]
             for t in range(5):
                 remote[g, p * BP + 8 * t : p * BP + 8 * t + 8, :] = value[t]
 
-    for k in range(5):
+    for k in range(4):
         pick[k, HALF:E, :] = jnp.zeros((HALF, 4 * E), bf16)
         pick[k, E + HALF : 2 * E, :] = jnp.zeros((HALF, 4 * E), bf16)
 
-    row = min_finish(2)
-    min_start(3, row)
-    from_all(lambda k, where: halo_copy(2, k, where).wait_recv())
-    for n in range(5):
-        blocks = [got_b[k, n] for k in range(4)] + [sent_b[n]]
-        total = gather([jnp.concatenate([x, swap(x)], axis=0) for x in blocks], slice(0, 4 * E))
-        for half in range(2 if n < 4 else 1):
-            rows = slice((2 * n + half) * BP, (2 * n + half + 1) * BP)
-            for g in range(4):
-                value = total[half * BP : (half + 1) * BP, g * E : (g + 1) * E]
-                remote[g, rows, :] = remote[g, rows, :] + value
-
-    def last_face(g, carry):
-        near(lambda p, j: remote[g, p * BP + j : p * BP + j + 1, :], B, g, g)
-        return carry
-
-    lax.fori_loop(0, 4, last_face, 0)
+    for chunk, (start, stop) in enumerate(LAST):
+        from_all(lambda k, where: halo_copy(2, chunk, k, where).wait_recv())
+        ps = range(2 * start, min(2 * stop, Q))
+        for n in range(start, stop):
+            blocks = [got_b[k, n] for k in range(4)]
+            total = gather([jnp.concatenate([x, swap(x)], axis=0) for x in blocks])
+            for half in range(2 if n < 4 else 1):
+                rows = slice((2 * n + half) * BP, (2 * n + half + 1) * BP)
+                for g in range(4):
+                    value = total[half * BP : (half + 1) * BP, g * E : (g + 1) * E]
+                    remote[g, rows, :] = remote[g, rows, :] + value
+
+        def last_face(g, carry, ps=ps):
+            sums = [jnp.zeros((BP, E), f32) for _ in ps]
+            sums = near(lambda p, j: remote[g, p * BP + j : p * BP + j + 1, :], 0, B, g, ps, sums)
+            for n, p in enumerate(ps):
+                applied[g, p] = sums[n]
+            return carry
+
+        lax.fori_loop(0, 4, last_face, 0)
     left_sums = contract(fine_weight(4), range(2), BP, nothing(BP))
     for q in range(Q):
         total = left_sums[q]
@@ -650,7 +693,8 @@
     def drain(k, where):
         side_copy(k, where).wait_send()
         for piece in range(3):
-            halo_copy(piece, k, where).wait_send()
+            for chunk in range(CHUNKS):
+                halo_copy(piece, chunk, k, where).wait_send()
 
     to_all(drain)
 
@@ -703,9 +747,10 @@
             vmem((1, E), f32),
             vmem((4, most, 1, E), f32),
             vmem((4, 4, E), jnp.int32),
-            vmem((2, Q, BP, E), f32),
+            vmem((Q, BP, E), f32),
+            vmem((Q, SENT, E), f32),
             vmem((5, BP, E), f32),
-            vmem((4, 2, Q, BP, E), f32),
+            vmem((4, Q, SENT, E), f32),
             vmem((4, 5, BP, E), f32),
             vmem((Q, 24, E), f32),
             vmem((Q, 16, E), f32),
@@ -716,25 +761,27 @@
             vmem((Q, BP, E), f32),
             vmem((7, E, E), f32),
             vmem((B * BP, E), f32),
-            vmem((Q, Q, 8, E), f32),
+            vmem((Q, Q, 24, E), f32),
             vmem((256, Q * E), bf16),
             vmem((72, E), f32),
             vmem((48, E), f32),
             vmem((24, E), f32),
             vmem((280, E), f32),
             vmem((11, Q, BP, E), f32),
-            vmem((5, Q, BP, E), f32),
+            vmem((2, Q, BP, E), f32),
+            vmem((2, Q, BP, E), f32),
             vmem((4, B * BP, E), f32),
-            vmem((5, 2 * E, 4 * E), bf16),
-            vmem((2, 4, Q * BP, E), f32),
+            vmem((4, 2 * E, 4 * E), bf16),
+            vmem((4, Q * HEIGHT[0], E), f32),
+            vmem((4, Q * HEIGHT[1], E), f32),
             vmem((4, Q * BP, E), f32),
             dma((14,)),
             dma((4, most)),
             dma((4, most)),
             dma((4,)),
             dma((4,)),
-            dma((3, 4)),
-            dma((3, 4)),
+            dma((3, CHUNKS, 4)),
+            dma((3, CHUNKS, 4)),
         ],
         compiler_params=pltpu.CompilerParams(
             collective_id=0, has_side_effects=True, vmem_limit_bytes=32 * 1024 * 1024

time: 41.7 us -> 40.3 us (0.966)
  Pallas kernels: 38.1 us -> 36.6 us
    pallas_call x1, Pallas kernels: 38.1 us -> 36.6 us  [shards(): call(*(pltpu.with_memory_space_constraint(x, pltpu.HBM) for x in operands))]
where the time goes in v3:
time: 40.3 us; the launch traced here: 40.1 us
  Pallas kernels  36.6 us (91%)
  between operations  2.33 us (6%)
  local copies, waits for them, and re-layouts  1.19 us (3%)
    pallas_call x1, Pallas kernels, shards(): call(*(pltpu.with_memory_space_constraint(x, pltpu.HBM) for x in operands))  36.6 us
    unnamed x2, local copies, waits for them, and re-layouts  1.19 us

profile of v3, /device:TPU:1, one launch (start us, length us, event | category | flops | bytes accessed | tf_op | source)
XLA Modules:
  0.0 40.1 jit_solution(8406153840252112326)
XLA Ops:
  0.6 36.6 %shard_map.157 = (f32[9,35,128]{2,1,0:T(8,128)S(1)}, f32[1,128]{1,0:T(1,128)S(1)}, f32[1,1]{1,0:T(1,128)}) custom-call(f32[9,35,128]{2,1,0:T(8,128)} %dof_in.1, f32[9,9,3,128]{3,2,1,0:T(4,128)} %bitcast.14, f32[2,9,9,4,128]{4,3,2,1,0:T(4,128)} %bitcast.13, f32[3,35,35]{2,1,0:T(8,128)} %stiff_in.1, f32[35,4,35]{2,1,0:T(4,128)} %bitcast.15, ...), custom_call_target="tpu_custom_call" | custom-call | tf_op jit(solution)/shard_map/pallas_call | solution.py:807
  37.3 0.7 %copy.20 = f32[9,35,128]{2,1,0:T(8,128)} copy(f32[9,35,128]{2,1,0:T(8,128)S(1)} %get-tuple-element.12) | data formatting | bytes 322560
  37.9 0.5 %copy.21 = f32[128]{0:T(128)} copy(f32[128]{0:T(128)S(1)} %bitcast.11) | data formatting | bytes 1024

commit v4 on v3

--- a/solution.py
+++ b/solution.py
@@ -87,6 +87,7 @@
     size,
     speed,
     rate,
+    mine,
     minima,
     side_got,
     dof,
@@ -151,6 +152,9 @@
         )
     ]
 
+    for load in loads[0:3]:
+        load.start()
+
     barrier = pltpu.get_barrier_semaphore()
     groups = {"depth": (d, n_depth), "strike": (s, n_strike)}
     order = sorted(range(1, max(n_depth, n_strike)), key=lambda off: abs(off - n_depth / 2))
@@ -160,7 +164,7 @@
                 pl.semaphore_signal(
                     barrier, inc=1, device_id={axis: lax.rem(me + off, count)}, device_id_type=MESH
                 )
-    for load in loads:
+    for load in loads[3:]:
         load.start()
 
     has = (s > 0, s < n_strike - 1, d > 0, d < n_depth - 1)
@@ -171,41 +175,48 @@
         (d > 0, {"depth": lax.rem(d + n_depth - 1, n_depth)}),
     )
 
-    def min_copy(stage, slot, off):
+    def min_copy(stage, off):
         axis = STAGES[stage]
         me, count = groups[axis]
         return pltpu.make_async_remote_copy(
-            src_ref=minima.at[stage, slot],
-            dst_ref=minima.at[stage, slot],
+            src_ref=mine.at[stage],
+            dst_ref=minima.at[stage, off - 1],
             send_sem=min_send.at[stage, off],
-            recv_sem=min_recv.at[stage, slot],
+            recv_sem=min_recv.at[stage],
             device_id={axis: lax.rem(me + off, count)},
             device_id_type=MESH,
         )
 
     def min_offsets(stage):
-        count = groups[STAGES[stage]][1]
-        return [off for off in order if off < count]
+        return [off for off in order if off < groups[STAGES[stage]][1]]
 
     def min_start(stage, row):
-        me, count = groups[STAGES[stage]]
-        minima[stage, me] = row
+        mine[stage] = row
         for off in min_offsets(stage):
-            min_copy(stage, me, off).start()
+            min_copy(stage, off).start()
 
     def min_finish(stage):
-        me, count = groups[STAGES[stage]]
-        for off in reversed(min_offsets(stage)):
-            min_copy(stage, lax.rem(me + off, count), off).wait_recv()
-        rows = [minima[stage, other] for other in range(count)]
+        axis = STAGES[stage]
+        me, count = groups[axis]
+        rows = [mine[stage]]
+        if count > 1:
+            others = minima.at[stage, pl.ds(0, count - 1)]
+            pltpu.make_async_remote_copy(
+                src_ref=others,
+                dst_ref=others,
+                send_sem=min_send.at[stage, 0],
+                recv_sem=min_recv.at[stage],
+                device_id={axis: lax.rem(me + 1, count)},
+                device_id_type=MESH,
+            ).wait_recv()
+            rows += [minima[stage, other] for other in range(count - 1)]
         while len(rows) > 1:
             rows = [jnp.minimum(a, b) for a, b in zip(rows[::2], rows[1::2])] + rows[len(rows) // 2 * 2 :]
         return rows[0]
 
     def min_drain(stage):
-        me, _ = groups[STAGES[stage]]
         for off in min_offsets(stage):
-            min_copy(stage, me, off).wait_send()
+            min_copy(stage, off).wait_send()
 
     def halo_copy(piece, chunk, k, where):
         if piece < 2:
@@ -329,7 +340,7 @@
                     sums[q] = sums[q] + weight(q, p, g) * field
             return tuple(sums)
 
-        if rows <= 16:
+        if rows <= 24:
             for p in range(Q):
                 sums = body(p, sums)
             return sums
@@ -634,8 +645,6 @@
         base = jnp.where(fine_left, middle[q], dof[q])
         middle[q] = base
 
-    row = min_finish(2)
-    min_start(3, row)
 
     coarse_halves = [
         jnp.where(left_row, coarse, swap(coarse)),
@@ -655,6 +664,15 @@
         pick[k, HALF:E, :] = jnp.zeros((HALF, 4 * E), bf16)
         pick[k, E + HALF : 2 * E, :] = jnp.zeros((HALF, 4 * E), bf16)
 
+    for stage in range(2):
+        min_drain(stage)
+    to_all(lambda k, where: side_copy(k, where).wait_send())
+    for piece in range(2):
+        for chunk in range(CHUNKS):
+            to_all(lambda k, where: halo_copy(piece, chunk, k, where).wait_send())
+
+    row = min_finish(2)
+    min_start(3, row)
     for chunk, (start, stop) in enumerate(LAST):
         from_all(lambda k, where: halo_copy(2, chunk, k, where).wait_recv())
         ps = range(2 * start, min(2 * stop, Q))
@@ -685,18 +703,11 @@
         value = part[0, q] + jnp.where(left_half, part[1, q], total + swap(total))
         dof_out[q] = (middle[q] + scaled(q, value, gain))[0:B]
 
+    min_drain(2)
+    for chunk in range(CHUNKS):
+        to_all(lambda k, where: halo_copy(2, chunk, k, where).wait_send())
     step_out[...] = COURANT * jnp.min(min_finish(3), axis=1, keepdims=True)
-
-    for stage in range(4):
-        min_drain(stage)
-
-    def drain(k, where):
-        side_copy(k, where).wait_send()
-        for piece in range(3):
-            for chunk in range(CHUNKS):
-                halo_copy(piece, chunk, k, where).wait_send()
-
-    to_all(drain)
+    min_drain(3)
 
 
 def shards(
@@ -745,7 +756,8 @@
             vmem((1, E), f32),
             vmem((1, E), f32),
             vmem((1, E), f32),
-            vmem((4, most, 1, E), f32),
+            vmem((4, 1, E), f32),
+            vmem((4, most - 1 if most > 1 else 1, 1, E), f32),
             vmem((4, 4, E), jnp.int32),
             vmem((Q, BP, E), f32),
             vmem((Q, SENT, E), f32),
@@ -777,7 +789,7 @@
             vmem((4, Q * BP, E), f32),
             dma((14,)),
             dma((4, most)),
-            dma((4, most)),
+            dma((4,)),
             dma((4,)),
             dma((4,)),
             dma((3, CHUNKS, 4)),

time: 40.3 us -> 39.4 us (0.978)
  Pallas kernels: 36.6 us -> 35.7 us
    pallas_call x1, Pallas kernels: 36.6 us -> 35.7 us  [shards(): call(*(pltpu.with_memory_space_constraint(x, pltpu.HBM) for x in operands))]
where the time goes in v4:
time: 39.4 us; the launch traced here: 39.2 us
  Pallas kernels  35.7 us (91%)
  between operations  2.33 us (6%)
  local copies, waits for them, and re-layouts  1.19 us (3%)
    pallas_call x1, Pallas kernels, shards(): call(*(pltpu.with_memory_space_constraint(x, pltpu.HBM) for x in operands))  35.7 us
    unnamed x2, local copies, waits for them, and re-layouts  1.19 us

profile of v4, /device:TPU:1, one launch (start us, length us, event | category | flops | bytes accessed | tf_op | source)
XLA Modules:
  0.0 39.2 jit_solution(18292119327163160029)
XLA Ops:
  0.6 35.7 %shard_map.157 = (f32[9,35,128]{2,1,0:T(8,128)S(1)}, f32[1,128]{1,0:T(1,128)S(1)}, f32[1,1]{1,0:T(1,128)}) custom-call(f32[9,35,128]{2,1,0:T(8,128)} %dof_in.1, f32[9,9,3,128]{3,2,1,0:T(4,128)} %bitcast.14, f32[2,9,9,4,128]{4,3,2,1,0:T(4,128)} %bitcast.13, f32[3,35,35]{2,1,0:T(8,128)} %stiff_in.1, f32[35,4,35]{2,1,0:T(4,128)} %bitcast.15, ...), custom_call_target="tpu_custom_call" | custom-call | tf_op jit(solution)/shard_map/pallas_call | solution.py:819
  36.3 0.7 %copy.20 = f32[9,35,128]{2,1,0:T(8,128)} copy(f32[9,35,128]{2,1,0:T(8,128)S(1)} %get-tuple-element.12) | data formatting | bytes 322560
  37.0 0.5 %copy.21 = f32[128]{0:T(128)} copy(f32[128]{0:T(128)S(1)} %bitcast.11) | data formatting | bytes 1024

commit v5 on v4

--- a/solution.py
+++ b/solution.py
@@ -396,9 +396,8 @@
         sent[q, 56:64, :] = series_1[q, 16:24] + jnp.where(sub8 >= 4, turned, 0.0)
         sent[q, 64:72, :] = jnp.where(sub8 < 4, turned, 0.0) + pltpu.roll(series_2[q, 8:16], 4, 0)
     sent[0, 32 + MARK : 33 + MARK, :] = coarse
-    for ks in ((0, 1), (2, 3)):
-        for chunk in range(CHUNKS):
-            to_all(lambda k, where: halo_copy(1, chunk, k, where).start(), ks)
+    for chunk in range(CHUNKS):
+        to_all(lambda k, where: halo_copy(1, chunk, k, where).start(), (0, 1))
 
     loads[8].wait()
 
@@ -466,6 +465,8 @@
     point()
     row = min_finish(0)
     min_start(1, row)
+    for chunk in range(CHUNKS):
+        to_all(lambda k, where: halo_copy(1, chunk, k, where).start(), (2, 3))
 
     loads[11].wait()
     selects = paired(select)

time: 39.4 us -> 39.4 us (level)
  no operation moved by 1% of the time
where the time goes in v5:
time: 39.4 us; the launch traced here: 39.3 us
  Pallas kernels  35.7 us (91%)
  between operations  2.33 us (6%)
  local copies, waits for them, and re-layouts  1.19 us (3%)
    pallas_call x1, Pallas kernels, shards(): call(*(pltpu.with_memory_space_constraint(x, pltpu.HBM) for x in operands))  35.7 us
    unnamed x2, local copies, waits for them, and re-layouts  1.19 us

profile of v5, /device:TPU:1, one launch (start us, length us, event | category | flops | bytes accessed | tf_op | source)
XLA Modules:
  0.0 39.3 jit_solution(14204686157201311576)
XLA Ops:
  0.6 35.7 %shard_map.157 = (f32[9,35,128]{2,1,0:T(8,128)S(1)}, f32[1,128]{1,0:T(1,128)S(1)}, f32[1,1]{1,0:T(1,128)}) custom-call(f32[9,35,128]{2,1,0:T(8,128)} %dof_in.1, f32[9,9,3,128]{3,2,1,0:T(4,128)} %bitcast.14, f32[2,9,9,4,128]{4,3,2,1,0:T(4,128)} %bitcast.13, f32[3,35,35]{2,1,0:T(8,128)} %stiff_in.1, f32[35,4,35]{2,1,0:T(4,128)} %bitcast.15, ...), custom_call_target="tpu_custom_call" | custom-call | tf_op jit(solution)/shard_map/pallas_call | solution.py:820
  36.4 0.7 %copy.20 = f32[9,35,128]{2,1,0:T(8,128)} copy(f32[9,35,128]{2,1,0:T(8,128)S(1)} %get-tuple-element.12) | data formatting | bytes 322560
  37.1 0.5 %copy.21 = f32[128]{0:T(128)} copy(f32[128]{0:T(128)S(1)} %bitcast.11) | data formatting | bytes 1024
